TPU v7x, 32 devices: a whole 2x2x4 slice. The times are simulated.
32 devices in a mesh: row: 4 (over x, core), col: 8 (over z, y).
Axes of the slice: x: 2, y: 2, z: 4, core: 2. Of those that a mesh axis runs over, the one named last changes fastest.
Arguments:
- field_rhs: float32 [4, 8, 2, 3, 512], P('row', 'col'), may hold values from -6 to 6
- positions: float32 [4, 8, 3, 512], P('row', 'col'), may hold values from 0.25 to 255.75, as said below
- polar: float32 [4, 8, 512], P('row', 'col'), may hold values from 0.5 to 4
- grid_base: int32 [4, 8, 3, 512], P('row', 'col'), may hold values from 0 to 255, as said below
- tile_lists: int32 [4, 8, 4, 12], P('row', 'col'), may hold values from 0 to 35, as said below
Outputs:
- dipoles: float32 [4, 8, 2, 3, 512], P('row', 'col')
- residual: float32 [4, 8, 2, 3, 512], P('row', 'col')
Inputs may be any that keep to these rules, and one draw needn't show every extreme that they name: grid_base + 2, modulo the grid's length in that dimension, is the grid cell holding the atom; the atoms of brick (r, c) lie in its cells r * 8 to r * 8 + 7 along x and c * 4 to c * 4 + 3 along y, no two atoms share a cell, and atom t * 128 + i of a brick lies in z cells t * 64 to (t + 1) * 64 - 1. positions minus the atom's cell lies in 0.25 to 0.75 in every dimension. `tile_lists`: entry k of tile t names a tile of the 3 x 3 bricks around the tile's own brick as value = b * 4 + tile with brick offset (b // 3 - 1, b mod 3 - 1); entry 0 is tile t itself (b = 4); the entries of one list are distinct, and each other entry is tile t - 1, t or t + 1 (modulo 4) of its brick.
All inputs are finite; a program needn't handle non-finite values.
Results may differ from a plain program's by a relative error of at most 0.0003.
Values sent between devices are 32-bit elements; how exact they have to be, the bound alone decides.
No kernel may reach another device: no remote copies, remote signals or barrier semaphores. Data moves between devices by JAX's collectives and lax.ppermute only.
A program may use at most 64 MiB of HBM per device.

v0:
```python
import math

import jax
import jax.numpy as jnp
import ml_dtypes
import numpy as np
from jax import lax
from jax.experimental import pallas as pl
from jax.experimental.pallas import tpu as pltpu
from jax.sharding import PartitionSpec as P

CX = 8
CY = 4
KZ = 256
TILE = 128
RHS = 2
ITERS = 2


ewald_beta = 0.4
thole_a = 0.39
self_coef = 4.0 * ewald_beta**3 / (3.0 * math.sqrt(math.pi))
highest = lax.Precision.HIGHEST


def with_halo(cells, sides, width):
    for axis, dim in sides:
        count = lax.axis_size(axis)
        head = lax.slice_in_dim(cells, 0, width, axis=dim)
        tail = lax.slice_in_dim(cells, cells.shape[dim] - width, cells.shape[dim], axis=dim)
        cells = jnp.concatenate(
            [
                lax.ppermute(tail, axis, [(i, (i + 1) % count) for i in range(count)]),
                cells,
                lax.ppermute(head, axis, [((i + 1) % count, i) for i in range(count)]),
            ],
            axis=dim,
        )
    return cells


def spline_table(fraction):
    previous = {0: jnp.ones_like(fraction)}
    fourth = previous
    for degree in range(2, 6):
        current = {}
        for offset in range(degree):
            abscissa = fraction + offset
            summed = abscissa * previous.get(offset, 0.0) + (degree - abscissa) * previous.get(
                offset - 1, 0.0
            )
            current[offset] = summed / (degree - 1)
        if degree == 4:
            fourth = current
        previous = current
    values = jnp.stack([previous[4 - stencil] for stencil in range(5)])
    slopes = jnp.stack(
        [fourth.get(4 - stencil, 0.0) - fourth.get(3 - stencil, 0.0) for stencil in range(5)]
    )
    return (values, slopes)


def spline_modulus(wave_index, length):
    spline_coef = (1.0 / 24.0, 11.0 / 24.0, 11.0 / 24.0, 1.0 / 24.0)
    cosine_sum = jnp.zeros(wave_index.shape, jnp.float32)
    sine_sum = jnp.zeros(wave_index.shape, jnp.float32)
    for offset in range(4):
        angles = 2.0 * math.pi / length * (wave_index * offset % length).astype(jnp.float32)
        cosine_sum = cosine_sum + spline_coef[offset] * jnp.cos(angles)
        sine_sum = sine_sum + spline_coef[offset] * jnp.sin(angles)
    return cosine_sum * cosine_sum + sine_sum * sine_sum


def folded_square(wave_index, length):
    nearest = jnp.minimum(wave_index, length - wave_index).astype(jnp.float32) / length
    return nearest * nearest


def influence(wave_x, wave_y, wave_z, length_x, length_y, length_z):
    wave_norm = (
        folded_square(wave_x, length_x)
        + folded_square(wave_y, length_y)
        + folded_square(wave_z, length_z)
    )
    modulus = (
        spline_modulus(wave_x, length_x)
        * spline_modulus(wave_y, length_y)
        * spline_modulus(wave_z, length_z)
    )
    excluded = (wave_x * 2 == length_x) | (wave_y * 2 == length_y) | (wave_z * 2 == length_z)
    excluded = excluded | (wave_x == 0) & (wave_y == 0) & (wave_z == 0)
    safe_norm = jnp.where(excluded, 1.0, wave_norm)
    safe_modulus = jnp.where(excluded, 1.0, modulus)
    result = jnp.exp(-(math.pi**2 / ewald_beta**2) * safe_norm) / (
        math.pi * safe_norm * safe_modulus
    )
    return jnp.where(excluded, 0.0, result)


def tile_field(own_static, near_static, near_dipole, box_spans):
    listed_count = near_static.shape[0]
    tile_width = own_static.shape[1]
    box_span = jnp.array(box_spans, dtype=jnp.float32)[None, :, None, None]
    separation = near_static[:, 0:3, None, :] - own_static[None, 0:3, :, None]
    separation = separation - box_span * jnp.floor(separation / box_span + 0.5)
    dist_sq = jnp.sum(separation * separation, axis=1)
    itself = (jnp.arange(listed_count)[:, None, None] == 0) & (
        jnp.arange(tile_width)[:, None] == jnp.arange(tile_width)[None, :]
    )[None]
    safe_sq = jnp.where(itself, 1.0, dist_sq)
    distance = jnp.sqrt(safe_sq)
    scaled = distance / (own_static[3][None, :, None] * near_static[:, 3][:, None, :])
    cubed = thole_a * scaled * scaled * scaled
    damping = jnp.exp(-cubed)
    screen = lax.erfc(ewald_beta * distance)
    gaussian = 2.0 * ewald_beta / math.sqrt(math.pi) * jnp.exp(-(ewald_beta * ewald_beta) * safe_sq)
    inverse_sq = 1.0 / safe_sq
    inverse_cube = inverse_sq / distance
    first_term = (screen - damping) * inverse_cube + gaussian * inverse_sq
    second = (
        3.0 * (screen - (1.0 + cubed) * damping) * inverse_cube * inverse_sq
        + gaussian * (2.0 * ewald_beta * ewald_beta + 3.0 * inverse_sq) * inverse_sq
    )
    first_term = jnp.where(itself, 0.0, first_term)
    second = jnp.where(itself, 0.0, second)
    projected = jnp.sum(near_dipole[:, :, :, None, :] * separation[:, None, :, :, :], axis=2)
    weighted = second[:, None] * projected
    outward = jnp.sum(weighted[:, :, None] * separation[:, None], axis=(0, 4))
    inward = jnp.sum(first_term[:, None, None] * near_dipole[:, :, :, None, :], axis=(0, 4))
    return outward - inward


def hartley(length):
    counter = jnp.arange(length, dtype=jnp.int32)
    angles = (
        2.0 * math.pi / length * (counter[:, None] * counter[None, :] % length).astype(jnp.float32)
    )
    return jnp.cos(angles) + jnp.sin(angles)


def placed_table(first_cell, weights, extent):
    slot_index = jnp.arange(extent, dtype=jnp.int32)[:, None]
    placed = jnp.zeros((extent, first_cell.shape[0]), jnp.float32)
    for stencil in range(5):
        placed = placed + jnp.where(
            slot_index == (first_cell[None, :] + stencil) % extent, weights[stencil][None, :], 0.0
        )
    return placed


def pad_axis(source, axis_pos, leading, trailing):
    widths = [(0, 0)] * source.ndim
    widths[axis_pos] = (leading, trailing)
    return jnp.pad(source, widths)


def fold_cycle(cycle_only, axis_pos, inner_len):
    middle = lax.slice_in_dim(cycle_only, 4, inner_len + 4, axis=axis_pos)
    lower_cycle = lax.slice_in_dim(cycle_only, 0, 2, axis=axis_pos)
    upper_cycle = lax.slice_in_dim(cycle_only, inner_len + 6, inner_len + 8, axis=axis_pos)
    return (
        middle
        + pad_axis(lower_cycle, axis_pos, 0, inner_len - 2)
        + pad_axis(upper_cycle, axis_pos, inner_len - 2, 0)
    )


def clear_inside(extended, extents):
    inside = None
    for axis_pos, inner_len in extents:
        slot_index = lax.broadcasted_iota(jnp.int32, extended.shape, axis_pos)
        within = (slot_index >= 2) & (slot_index < inner_len + 6)
        inside = within if inside is None else inside & within
    return jnp.where(inside, 0.0, extended)


def inner_sum(left_arr, right_arr):
    return lax.psum(jnp.sum(left_arr * right_arr, axis=(1, 2)), ("row", "col"))


def pencil_local(field_rhs, positions, polar, grid_base, tile_lists):
    rows_count = lax.axis_size("row")
    cols_count = lax.axis_size("col")
    grid_x = CX * rows_count
    grid_y = CY * cols_count
    atom_count = polar.shape[-1]
    tile_count = atom_count // TILE
    slab_depth = KZ // tile_count
    window_len = slab_depth + 4
    box_spans = (float(grid_x), float(grid_y), float(KZ))
    own_place = positions[0, 0]
    own_base = grid_base[0, 0]
    own_polar = polar[0, 0]
    lengths = jnp.array([grid_x, grid_y, KZ], dtype=jnp.int32)[:, None]
    cell_index = (own_base + 2) % lengths
    fraction = own_place - cell_index.astype(jnp.float32)
    values, slopes = spline_table(fraction)
    first_x = (own_base[0] - lax.axis_index("row") * CX + 2) % grid_x
    first_y = (own_base[1] - lax.axis_index("col") * CY + 2) % grid_y
    rows_x = placed_table(first_x, values[:, 0], CX + 4)
    slope_x = placed_table(first_x, slopes[:, 0], CX + 4)
    rows_y = placed_table(first_y, values[:, 1], CY + 4)
    slope_y = placed_table(first_y, slopes[:, 1], CY + 4)
    tile_start = jnp.arange(atom_count, dtype=jnp.int32) // TILE * slab_depth
    first_z = (own_base[2] + 2 - tile_start) % KZ
    rows_z = placed_table(first_z, values[:, 2], window_len)
    slope_z = placed_table(first_z, slopes[:, 2], window_len)
    plane_count = (CX + 4) * (CY + 4)
    plane_dx = (slope_x[:, None, :] * rows_y[None, :, :]).reshape(plane_count, atom_count)
    plane_dy = (rows_x[:, None, :] * slope_y[None, :, :]).reshape(plane_count, atom_count)
    plane_flat = (rows_x[:, None, :] * rows_y[None, :, :]).reshape(plane_count, atom_count)
    window_rows = jnp.moveaxis(rows_z.reshape(window_len, tile_count, TILE), 1, 0)
    window_slope = jnp.moveaxis(slope_z.reshape(window_len, tile_count, TILE), 1, 0)
    depth_table = jnp.concatenate([window_rows, window_slope], axis=2)
    grid_scale = 1.0 / (grid_x * grid_y * KZ)
    hartley_x = hartley(grid_x)
    hartley_y = hartley(grid_y)
    hartley_z = hartley(KZ)
    block_y = grid_y // rows_count
    block_z = KZ // cols_count
    wave_x = jnp.arange(grid_x, dtype=jnp.int32)[:, None, None]
    wave_y = (lax.axis_index("row") * block_y + jnp.arange(block_y, dtype=jnp.int32))[None, :, None]
    wave_z = (lax.axis_index("col") * block_z + jnp.arange(block_z, dtype=jnp.int32))[None, None, :]
    kernel = influence(wave_x, wave_y, wave_z, grid_x, grid_y, KZ) * grid_scale
    root_scale = jnp.power(own_polar, 1.0 / 6.0)
    own_static = jnp.concatenate([own_place, root_scale[None]], axis=0)
    near_static = with_halo(own_static[None, None], (("row", 0), ("col", 1)), 1)
    near_static = jnp.moveaxis(near_static.reshape(9, 4, tile_count, TILE), 2, 1).reshape(
        9 * tile_count, 4, TILE
    )
    own_tiles = jnp.moveaxis(own_static.reshape(4, tile_count, TILE), 1, 0)
    own_lists = tile_lists[0, 0]
    polar_wide = own_polar[None, None, :]
    solution = jnp.zeros_like(field_rhs[0, 0])
    residual = field_rhs[0, 0]
    scaled_res = polar_wide * residual
    direction = scaled_res
    progress = inner_sum(residual, scaled_res)
    for iteration in range(ITERS):
        near_dip = with_halo(direction[None, None], (("row", 0), ("col", 1)), 1)
        near_dip = jnp.moveaxis(near_dip.reshape(9, RHS, 3, tile_count, TILE), 3, 1).reshape(
            9 * tile_count, RHS, 3, TILE
        )

        def one_tile(tile_pos):
            picked = own_lists[tile_pos]
            return tile_field(own_tiles[tile_pos], near_static[picked], near_dip[picked], box_spans)

        fields = lax.map(one_tile, jnp.arange(tile_count, dtype=jnp.int32))
        direct = jnp.moveaxis(fields, 0, 2).reshape(RHS, 3, atom_count)
        slope_terms = (
            direction[:, 0, None, :] * plane_dx[None] + direction[:, 1, None, :] * plane_dy[None]
        )
        flat_terms = direction[:, 2, None, :] * plane_flat[None]
        spread_left = jnp.concatenate(
            [
                slope_terms.reshape(RHS, plane_count, tile_count, TILE),
                flat_terms.reshape(RHS, plane_count, tile_count, TILE),
            ],
            axis=3,
        )
        spread_windows = jnp.einsum("sptb,twb->sptw", spread_left, depth_table, precision=highest)
        main_part = spread_windows[..., :slab_depth].reshape(spread_windows.shape[:-2] + (KZ,))
        tail_part = pad_axis(
            spread_windows[..., slab_depth:], spread_windows.ndim - 1, 0, slab_depth - 4
        )
        tail_part = tail_part.reshape(spread_windows.shape[:-2] + (KZ,))[..., : KZ + 4 - slab_depth]
        last_axis = main_part.ndim - 1
        padded_line = pad_axis(main_part, last_axis, 0, 4) + pad_axis(
            tail_part, last_axis, slab_depth, 0
        )
        inner = padded_line[..., 2 : KZ + 2]
        spread_tile = (
            inner
            + pad_axis(padded_line[..., 0:2], last_axis, KZ - 2, 0)
            + pad_axis(padded_line[..., KZ + 2 : KZ + 4], last_axis, 0, KZ - 2)
        ).reshape(RHS, CX + 4, CY + 4, KZ)
        extended = with_halo(spread_tile, (("row", 1), ("col", 2)), 2)
        cycle_only = clear_inside(extended, ((1, CX), (2, CY)))
        folded = fold_cycle(fold_cycle(cycle_only, 1, CX), 2, CY)
        spectrum = jnp.einsum(
            "sxyz,zk->sxyk",
            spread_tile[:, 2 : CX + 2, 2 : CY + 2] + folded,
            hartley_z,
            precision=highest,
        )
        along_y = jnp.einsum(
            "sxyz,yk->sxkz",
            lax.all_to_all(spectrum, "col", split_axis=3, concat_axis=2, tiled=True),
            hartley_y,
            precision=highest,
        )
        along_x = (
            jnp.einsum(
                "sxyz,xk->skyz",
                lax.all_to_all(along_y, "row", split_axis=2, concat_axis=1, tiled=True),
                hartley_x,
                precision=highest,
            )
            * kernel[None]
        )
        mixed_part = jnp.einsum("sxyz,xk->skyz", along_x, hartley_x, precision=highest)
        returned = lax.all_to_all(mixed_part, "row", split_axis=1, concat_axis=2, tiled=True)
        swapped = jnp.einsum("sxyz,yk->sxkz", returned, hartley_y, precision=highest)
        restored = lax.all_to_all(swapped, "col", split_axis=2, concat_axis=3, tiled=True)
        padded = with_halo(
            jnp.einsum("sxyz,zk->sxyk", restored, hartley_z, precision=highest),
            (("row", 1), ("col", 2)),
            2,
        )
        line = padded.reshape(RHS, plane_count, KZ)
        extended_line = jnp.concatenate([line[..., KZ - 2 :], line, line[..., :2]], axis=-1)
        windows = jnp.stack(
            [
                extended_line[..., tile * slab_depth : tile * slab_depth + window_len]
                for tile in range(tile_count)
            ],
            axis=-2,
        )
        sampled = jnp.einsum("sptw,twb->sptb", windows, depth_table, precision=highest)
        with_flat = sampled[..., :TILE].reshape(RHS, plane_count, atom_count)
        with_slope = sampled[..., TILE:].reshape(RHS, plane_count, atom_count)
        recip_part = jnp.stack(
            [
                jnp.sum(with_flat * plane_dx[None], axis=1),
                jnp.sum(with_flat * plane_dy[None], axis=1),
                jnp.sum(with_slope * plane_flat[None], axis=1),
            ],
            axis=1,
        )
        image_field = direction / polar_wide - direct + recip_part - self_coef * direction
        step_size = (progress / inner_sum(direction, image_field))[:, None, None]
        solution = solution + step_size * direction
        residual = residual - step_size * image_field
        scaled_res = polar_wide * residual
        progress_next = inner_sum(residual, scaled_res)
        direction = scaled_res + (progress_next / progress)[:, None, None] * direction
        progress = progress_next
    return (solution[None, None], residual[None, None])


X_PAD = CX + 4
Y_PAD = CY + 4
SLOT_ROWS = 16
SPLIT = 2
VMEM_LIMIT = 60_000_000
SMALL_VMEM_LIMIT = 24_000_000
EARLY_TILES = 1
PAIR_ROWS = 32
GROUP = 8
SCREEN_SCALE = 0.4
SCREEN_COEF = (
    0.22567588090896606,
    0.2256690263748169,
    0.20785020291805267,
    0.16849851608276367,
    0.14156343042850494,
    -0.005832736846059561,
    0.16930203139781952,
    -0.1830107867717743,
    0.05028456076979637,
)


def halves(value):
    high = value.astype(jnp.bfloat16)
    return high, (value - high.astype(jnp.float32)).astype(jnp.bfloat16)


def halves_np(value):
    value = value.astype(np.float32)
    high = value.astype(ml_dtypes.bfloat16)
    return high, (value - high.astype(np.float32)).astype(ml_dtypes.bfloat16)


def product(left, right, left_dim=1, right_dim=0):
    def one(first, second):
        return lax.dot_general(
            first,
            second,
            (((left_dim,), (right_dim,)), ((), ())),
            preferred_element_type=jnp.float32,
        )

    return one(left[0], right[0]) + (one(left[1], right[0]) + one(left[0], right[1]))


def cas_np(wave, place, length):
    angles = 2.0 * np.pi / length * (wave[:, None] * place[None, :] % length)
    return np.cos(angles) + np.sin(angles)


def modulus_np(wave, length):
    coef = np.array([1.0, 11.0, 11.0, 1.0]) / 24.0
    angles = 2.0 * np.pi / length * (wave[:, None] * np.arange(4)[None, :])
    return (coef * np.cos(angles)).sum(1) ** 2 + (coef * np.sin(angles)).sum(1) ** 2


def influence_np(length_x, length_y, length_z):
    total = np.zeros((length_x, length_y, length_z))
    modulus = np.ones((length_x, length_y, length_z))
    excluded = np.zeros((length_x, length_y, length_z), bool)
    for axis, length in enumerate((length_x, length_y, length_z)):
        wave = np.arange(length)
        shape = [1, 1, 1]
        shape[axis] = length
        total = total + ((np.minimum(wave, length - wave) / length) ** 2).reshape(shape)
        modulus = modulus * modulus_np(wave, length).reshape(shape)
        excluded = excluded | (wave * 2 == length).reshape(shape)
    excluded[0, 0, 0] = True
    safe = np.where(excluded, 1.0, total)
    result = np.exp(-(np.pi**2) / ewald_beta**2 * safe) / (
        np.pi * safe * np.where(excluded, 1.0, modulus)
    )
    return np.where(excluded, 0.0, result) / (length_x * length_y * length_z)


def slab_tables(rows_count, cols_count):
    grid_x = CX * rows_count
    grid_y = CY * cols_count
    devices = rows_count * cols_count
    chunk = KZ // devices
    wave_z = (np.arange(devices)[None, :] * chunk + np.arange(chunk)[:, None]).reshape(-1)
    along_z = cas_np(wave_z, np.arange(KZ), KZ)
    place_x = np.arange(rows_count)[:, None] * CX + np.arange(X_PAD)[None, :] - 2
    along_x = cas_np(np.arange(grid_x), place_x.reshape(-1) % grid_x, grid_x)
    x_high, x_low = halves_np(along_x)
    forward_x = np.concatenate([x_high, x_low, x_high], axis=1)
    backward_x = np.concatenate([x_high.T, x_low.T, x_high.T], axis=1)
    place_y = (np.arange(cols_count)[:, None] * CY + np.arange(Y_PAD)[None, :] - 2) % grid_y
    along_y = cas_np(np.arange(grid_y), place_y.reshape(-1), grid_y)
    along_y = along_y.reshape(grid_y, cols_count, Y_PAD)
    units = chunk * RHS // SPLIT
    block = np.einsum("uv,kcy->cuyvk", np.eye(units), along_y)
    block = block.reshape(cols_count * units * Y_PAD, units * grid_y)
    kernel = influence_np(grid_x, grid_y, KZ).reshape(grid_x, grid_y, devices, chunk)
    kernel = np.transpose(kernel, (2, 0, 3, 1))[:, :, :, None, :]
    kernel = np.broadcast_to(kernel, (devices, grid_x, chunk, RHS, grid_y))
    kernel = kernel.reshape(devices, grid_x, SPLIT, units * grid_y)
    kernel = np.moveaxis(kernel, 2, 1).reshape(devices, SPLIT * grid_x, units * grid_y)
    kernel = kernel.astype(np.float32)
    return dict(
        along_z=halves_np(along_z),
        forward_x=forward_x,
        backward_x=backward_x,
        block=halves_np(block),
        kernel=kernel,
    )


def pack_body(rhs_ref, place_ref, polar_ref, start_ref, payload_ref):
    polar = polar_ref[...]
    start = read_rows(rhs_ref) * polar
    start_ref[...] = start
    place = [place_ref[dim] for dim in range(3)]
    everything = jnp.concatenate(place + [1.0 / jnp.sqrt(polar), start], axis=0)
    store_payload(payload_ref, everything)


def read_rows(rows_ref):
    return jnp.concatenate([rows_ref[dim] for dim in range(3)], axis=0)


def store_payload(payload_ref, everything):
    tile_count = everything.shape[1] // TILE
    for quantity in range(everything.shape[0]):
        for tile in range(tile_count):
            row = quantity * tile_count + tile
            payload_ref[row : row + 1, :] = everything[
                quantity : quantity + 1, tile * TILE : (tile + 1) * TILE
            ]


def placed_rows(slot, weights, extent):
    slot_index = lax.broadcasted_iota(jnp.int32, (extent, slot.shape[1]), 0)
    placed = jnp.zeros((extent, slot.shape[1]), jnp.float32)
    for stencil in range(5):
        target = slot + stencil
        if extent == KZ:
            target = jnp.where(target >= KZ, target - KZ, target)
        placed = placed + jnp.where(slot_index == target, weights[stencil], 0.0)
    return placed


def spread_into(message_ref, moment, rows_x, slope_x, rows_y, slope_y, depth, devices):
    blocks = []
    for step in range(X_PAD):
        flat_x = rows_x[step : step + 1]
        tilt_x = slope_x[step : step + 1]
        for rhs in range(RHS):
            part_x = tilt_x * moment[rhs : rhs + 1]
            part_y = flat_x * moment[RHS + rhs : RHS + rhs + 1]
            part_z = flat_x * moment[2 * RHS + rhs : 2 * RHS + rhs + 1]
            blocks.append(
                jnp.concatenate([part_x * rows_y + part_y * slope_y, part_z * rows_y], axis=1)
            )
    charges = jnp.concatenate(blocks, axis=0)
    spectrum = product(depth, halves(charges), 1, 1)
    slot_rows = message_ref.shape[0] // devices
    chunk = KZ // devices
    width = RHS * Y_PAD
    for step in range(X_PAD):
        message_ref[pl.ds(step, devices, stride=slot_rows), :] = jnp.concatenate(
            [
                spectrum[unit * devices : (unit + 1) * devices, step * width : (step + 1) * width]
                for unit in range(chunk)
            ],
            axis=1,
        )


def sample_from(message_ref, rows_x, slope_x, rows_y, slope_y, depth, devices):
    chunk = KZ // devices
    width = RHS * Y_PAD
    slot_rows = message_ref.shape[0] // devices
    pieces = [
        message_ref[pl.ds(step, devices, stride=slot_rows), :] for step in range(X_PAD)
    ]
    spare = jnp.zeros((devices, KZ - X_PAD * width), jnp.float32)
    spectrum = jnp.concatenate(
        [
            jnp.concatenate(
                [piece[:, unit * width : (unit + 1) * width] for piece in pieces] + [spare], axis=1
            )
            for unit in range(chunk)
        ],
        axis=0,
    )
    spectrum = jnp.transpose(spectrum)[: X_PAD * width]
    sampled = product(halves(spectrum), depth, 1, 0)
    atoms = rows_x.shape[1]
    fields = [None] * (3 * RHS)
    for rhs in range(RHS):
        sum_x = sum_y = sum_z = None
        for step in range(X_PAD):
            first = step * width + rhs * Y_PAD
            flat = sampled[first : first + Y_PAD, :atoms]
            tilt = sampled[first : first + Y_PAD, atoms:]
            part_x = slope_x[step : step + 1] * flat
            part_y = rows_x[step : step + 1] * flat
            part_z = rows_x[step : step + 1] * tilt
            sum_x = part_x if sum_x is None else sum_x + part_x
            sum_y = part_y if sum_y is None else sum_y + part_y
            sum_z = part_z if sum_z is None else sum_z + part_z
        fields[rhs] = jnp.sum(sum_x * rows_y, axis=0, keepdims=True)
        fields[RHS + rhs] = jnp.sum(sum_y * slope_y, axis=0, keepdims=True)
        fields[2 * RHS + rhs] = jnp.sum(sum_z * rows_y, axis=0, keepdims=True)
    return jnp.concatenate(fields, axis=0)


def read_tables(tables_ref):
    return (
        tables_ref[0:X_PAD],
        tables_ref[SLOT_ROWS : SLOT_ROWS + X_PAD],
        tables_ref[2 * SLOT_ROWS : 2 * SLOT_ROWS + Y_PAD],
        tables_ref[2 * SLOT_ROWS + Y_PAD : 2 * SLOT_ROWS + 2 * Y_PAD],
    )


def setup_body(
    lengths,
    devices,
    place_ref,
    base_ref,
    start_ref,
    z_high_ref,
    z_low_ref,
    message_ref,
    tables_ref,
    depth_high_ref,
    depth_low_ref,
):
    base = [base_ref[dim] for dim in range(3)]
    fractions = []
    cells = []
    for dim in range(3):
        cell = base[dim] + 2
        cell = jnp.where(cell >= lengths[dim], cell - lengths[dim], cell)
        cells.append(cell)
        fractions.append(place_ref[dim] - cell.astype(jnp.float32))
    values, slopes = spline_table(jnp.concatenate(fractions, axis=0))
    values = [[values[stencil][dim : dim + 1] for stencil in range(5)] for dim in range(3)]
    slopes = [[slopes[stencil][dim : dim + 1] for stencil in range(5)] for dim in range(3)]
    slot_x = lax.rem(cells[0], CX)
    slot_y = lax.rem(cells[1], CY)
    tables_ref[0:SLOT_ROWS] = placed_rows(slot_x, values[0], SLOT_ROWS)
    tables_ref[SLOT_ROWS : 2 * SLOT_ROWS] = placed_rows(slot_x, slopes[0], SLOT_ROWS)
    tables_ref[2 * SLOT_ROWS : 2 * SLOT_ROWS + Y_PAD] = placed_rows(slot_y, values[1], Y_PAD)
    tables_ref[2 * SLOT_ROWS + Y_PAD : 2 * SLOT_ROWS + 2 * Y_PAD] = placed_rows(
        slot_y, slopes[1], Y_PAD
    )
    window = jnp.concatenate(
        [
            placed_rows(base[2], values[2], KZ),
            placed_rows(base[2], slopes[2], KZ),
        ],
        axis=1,
    )
    depth = product((z_high_ref[...], z_low_ref[...]), halves(window), 1, 0)
    depth = halves(depth)
    depth_high_ref[...] = depth[0]
    depth_low_ref[...] = depth[1]
    spread_into(message_ref, start_ref[...], *read_tables(tables_ref), depth, devices)


def transform_in(message_ref, forward_ref, block_high_ref, block_low_ref, rows_count, cols_count):
    gathered = jnp.concatenate(
        [
            jnp.concatenate(
                [
                    message_ref[(r * cols_count + c) * X_PAD : (r * cols_count + c + 1) * X_PAD]
                    for r in range(rows_count)
                ],
                axis=0,
            )
            for c in range(cols_count)
        ],
        axis=1,
    )
    high, low = halves(gathered)
    along = jnp.dot(
        forward_ref[...],
        jnp.concatenate([high, high, low], axis=0),
        preferred_element_type=jnp.float32,
    )
    part = along.shape[1] // cols_count // SPLIT
    along = jnp.concatenate(
        [
            jnp.concatenate(
                [
                    along[:, (c * SPLIT + half) * part : (c * SPLIT + half + 1) * part]
                    for c in range(cols_count)
                ],
                axis=1,
            )
            for half in range(SPLIT)
        ],
        axis=0,
    )
    return product(halves(along), (block_high_ref[...], block_low_ref[...]))


def transform_out(result_ref, values, backward_ref, block_high_ref, block_low_ref, counts):
    rows_count, cols_count = counts
    spread = product(halves(values), (block_high_ref[...], block_low_ref[...]), 1, 1)
    grid_x = spread.shape[0] // SPLIT
    part = spread.shape[1] // cols_count
    spread = jnp.concatenate(
        [
            spread[half * grid_x : (half + 1) * grid_x, c * part : (c + 1) * part]
            for c in range(cols_count)
            for half in range(SPLIT)
        ],
        axis=1,
    )
    high, low = halves(spread)
    along = jnp.dot(
        backward_ref[...],
        jnp.concatenate([high, high, low], axis=0),
        preferred_element_type=jnp.float32,
    )
    width = along.shape[1] // cols_count
    slot_rows = result_ref.shape[0] // (rows_count * cols_count)
    for r in range(rows_count):
        for c in range(cols_count):
            first = (r * cols_count + c) * slot_rows
            result_ref[first : first + X_PAD, :] = along[
                r * X_PAD : (r + 1) * X_PAD, c * width : (c + 1) * width
            ]


def middle_first_body(
    counts,
    message_ref,
    kernel_ref,
    forward_ref,
    backward_ref,
    block_high_ref,
    block_low_ref,
    result_ref,
    wave_ref,
):
    wave = transform_in(message_ref, forward_ref, block_high_ref, block_low_ref, *counts)
    wave_ref[...] = wave
    transform_out(
        result_ref, wave * kernel_ref[...], backward_ref, block_high_ref, block_low_ref, counts
    )


def gather_rows(parts):
    tiles = [
        parts[GROUP * tile : GROUP * tile + GROUP, :] for tile in range(parts.shape[0] // GROUP)
    ]
    return jnp.concatenate(tiles, axis=1)[0 : 3 * RHS]


def row_total(value, rhs):
    row = lax.broadcasted_iota(jnp.int32, value.shape, 0)
    return total(jnp.where(lax.rem(row, RHS) == rhs, value, 0.0))


def total(value):
    return jnp.sum(jnp.sum(value, axis=0, keepdims=True), axis=1, keepdims=True)


def middle_second_body(
    counts,
    message_ref,
    kernel_ref,
    forward_ref,
    backward_ref,
    block_high_ref,
    block_low_ref,
    wave_ref,
    rhs_ref,
    start_ref,
    image_ref,
    second_ref,
    near_ref,
    polar_ref,
    result_ref,
):
    rhs_rows = read_rows(rhs_ref)
    near_rows = gather_rows(near_ref)
    wave = transform_in(message_ref, forward_ref, block_high_ref, block_low_ref, *counts)
    filtered = wave * kernel_ref[...]
    transform_out(result_ref, filtered, backward_ref, block_high_ref, block_low_ref, counts)
    before = wave_ref[...]
    grid_y = CY * counts[1]
    lane = lax.broadcasted_iota(jnp.int32, wave.shape, 1)
    own_rhs = lax.rem(lax.div(lane, grid_y), RHS)
    second = second_ref[...]
    start = start_ref[...]
    image = image_ref[...]
    local_part = second / polar_ref[...] - near_rows - self_coef * second
    slot = lax.broadcasted_iota(jnp.int32, (1, result_ref.shape[1]), 1)
    sums = jnp.zeros((1, result_ref.shape[1]), jnp.float32)
    for rhs in range(RHS):
        mine = own_rhs == rhs
        parts = (
            row_total(rhs_rows * start, rhs),
            row_total(start * image, rhs),
            row_total(second * image, rhs),
            row_total(start * local_part, rhs) + total(jnp.where(mine, before * filtered, 0.0)),
            row_total(second * local_part, rhs) + total(jnp.where(mine, wave * filtered, 0.0)),
        )
        for index, part in enumerate(parts):
            sums = jnp.where(slot == rhs * len(parts) + index, part, sums)
    devices = counts[0] * counts[1]
    result_ref[pl.ds(X_PAD, devices, stride=X_PAD + 1), :] = jnp.broadcast_to(
        sums, (devices, sums.shape[1])
    )


def sample_body(
    devices,
    message_ref,
    tables_ref,
    depth_high_ref,
    depth_low_ref,
    start_ref,
    near_ref,
    polar_ref,
    image_ref,
    second_ref,
    payload_ref,
):
    tables = read_tables(tables_ref)
    depth = (depth_high_ref[...], depth_low_ref[...])
    field = sample_from(message_ref, *tables, depth, devices)
    start = start_ref[...]
    polar = polar_ref[...]
    image = start / polar - gather_rows(near_ref) + field - self_coef * start
    second = polar * image
    image_ref[...] = image
    second_ref[...] = second
    store_payload(payload_ref, second)


def spread_body(
    devices,
    tables_ref,
    depth_high_ref,
    depth_low_ref,
    second_ref,
    result_ref,
):
    depth = (depth_high_ref[...], depth_low_ref[...])
    spread_into(result_ref, second_ref[...], *read_tables(tables_ref), depth, devices)


def final_body(
    devices,
    message_ref,
    tables_ref,
    depth_high_ref,
    depth_low_ref,
    rhs_ref,
    start_ref,
    image_ref,
    second_ref,
    near_ref,
    polar_ref,
    dipole_ref,
    residual_ref,
):
    tables = read_tables(tables_ref)
    depth = (depth_high_ref[...], depth_low_ref[...])
    field = sample_from(message_ref, *tables, depth, devices)
    second = second_ref[...]
    start = start_ref[...]
    image = image_ref[...]
    image_second = second / polar_ref[...] - gather_rows(near_ref) + field - self_coef * second
    sums = jnp.sum(
        message_ref[pl.ds(X_PAD, devices, stride=X_PAD + 1), :], axis=0, keepdims=True
    )
    steps = []
    for rhs in range(RHS):
        progress, start_image, second_image, start_next, second_next = [
            sums[:, rhs * 5 + index : rhs * 5 + index + 1] for index in range(5)
        ]
        step = progress / start_image
        progress_next = progress - 2.0 * step * start_image + step * step * second_image
        grown = 1.0 + progress_next / progress
        curvature = (
            grown * grown * start_image
            - step * grown * (start_next + second_image)
            + step * step * second_next
        )
        steps.append((step, grown, progress_next / curvature))
    row = lax.broadcasted_iota(jnp.int32, (RHS, 1), 0)
    step, grown, step_next = [
        sum(jnp.where(row == rhs, steps[rhs][index], 0.0) for rhs in range(RHS))
        for index in range(3)
    ]
    for dim in range(3):
        rows = slice(dim * RHS, (dim + 1) * RHS)
        direction = grown * start[rows] - step * second[rows]
        image_direction = grown * image[rows] - step * image_second[rows]
        dipole_ref[dim] = step * start[rows] + step_next * direction
        residual_ref[dim] = rhs_ref[dim] - step * image[rows] - step_next * image_direction


def near_base(entry, brick_rows):
    return lax.shift_right_logical(entry, 2) * brick_rows + lax.bitwise_and(entry, 3)


def fill_near(scratch, up_ref, stack_ref, down_ref):
    rows = stack_ref.shape[0]
    scratch[0:rows, :] = up_ref[...]
    scratch[rows : 2 * rows, :] = stack_ref[...]
    scratch[2 * rows : 3 * rows, :] = down_ref[...]


def nearest(places, origin, span):
    return places - span * jnp.floor((places - origin) * (1.0 / span) + 0.5)


def unwrap_near(near, tile_count, spans):
    rows = near.shape[0] // 9
    for dim in range(2):
        own = 4 * rows + dim * tile_count
        origin = near[own : own + 1, 0:1]
        for brick in range(9):
            first = brick * rows + dim * tile_count
            near[first : first + tile_count, :] = nearest(
                near[first : first + tile_count, :], origin, spans[dim]
            )


def pick_rows(picked, near, lists_ref, tile, tile_count, quantities, origin, span):
    rows = near.shape[0] // 9
    for entry in range(lists_ref.shape[1]):
        base = near_base(lists_ref[tile, entry], rows)
        for quantity in range(quantities):
            values = near[pl.ds(base + quantity * tile_count, 1), :]
            if quantity == 2 and span is not None:
                values = nearest(values, origin, span)
            first = (entry * quantities + quantity) * GROUP
            picked[first : first + GROUP, :] = jnp.broadcast_to(values, (GROUP, TILE))


def widen_own(near, quantities, tile_count, tile, square, wide):
    offset = near.shape[0] // 9 * 4
    for quantity in range(quantities):
        square[quantity : quantity + 1, :] = near[
            pl.ds(offset + quantity * tile_count + tile, 1), :
        ]
    columns = jnp.transpose(square[...])
    for quantity in range(quantities):
        wide[quantity * TILE : (quantity + 1) * TILE, :] = jnp.broadcast_to(
            columns[:, quantity : quantity + 1], (TILE, TILE)
        )


def add_field(sums, first_term, second_term, apart, moments):
    for rhs in range(RHS):
        moment = [moments[RHS * dim + rhs] for dim in range(3)]
        projected = moment[0] * apart[0] + moment[1] * apart[1] + moment[2] * apart[2]
        weighted = second_term * projected
        for dim in range(3):
            index = RHS * dim + rhs
            sums[index] = sums[index] + (weighted * apart[dim] - first_term * moment[dim])


def finish_sums(field_ref, sums_ref):
    lane = lax.broadcasted_iota(jnp.int32, (TILE, TILE), 1)
    merged = jnp.zeros((TILE, TILE), jnp.float32)
    for index in range(3 * RHS):
        column = jnp.sum(sums_ref[index * TILE : (index + 1) * TILE, :], axis=1, keepdims=True)
        merged = jnp.where(lane == index, column, merged)
    field_ref[...] = jnp.transpose(merged)[0:GROUP]


def pair_rows(start, group):
    return pl.ds(pl.multiple_of(start + group * GROUP, GROUP), GROUP)


def wide_rows(start, group, quantity):
    return pl.ds(pl.multiple_of(quantity * TILE + start + group * GROUP, GROUP), GROUP)


def pair_terms(square_dist, damp):
    inverse = lax.rsqrt(square_dist)
    distance = square_dist * inverse
    inverse_sq = inverse * inverse
    inverse_cube = inverse_sq * inverse
    cubed = damp * (distance * square_dist)
    damping = jnp.exp(cubed)
    bell = jnp.exp(-(ewald_beta * ewald_beta) * square_dist)
    stretched = 1.0 + (SCREEN_SCALE * ewald_beta) * distance
    turned = pl.reciprocal(stretched, approx=True)
    turned = turned * (2.0 - stretched * turned)
    series = SCREEN_COEF[-1] * turned + SCREEN_COEF[-2]
    for coef in SCREEN_COEF[-3::-1]:
        series = series * turned + coef
    screen = bell * turned * series
    gaussian = (2.0 * ewald_beta / math.sqrt(math.pi)) * bell
    bare = screen - damping
    first_term = bare * inverse_cube + gaussian * inverse_sq
    second_term = (
        3.0 * (first_term + (cubed * damping) * inverse_cube)
        + (2.0 * ewald_beta * ewald_beta) * gaussian
    ) * inverse_sq
    return first_term, second_term


def pair_first_body(
    first_tile,
    tile_count,
    spans,
    lists_ref,
    up_ref,
    stack_ref,
    down_ref,
    *others,
):
    first_ref, second_ref, field_ref, near_ref, near, picked, square, wide, sums_ref = others[-9:]

    @pl.when(pl.program_id(0) == 0)
    def _():
        fill_near(near, up_ref, stack_ref, down_ref)
        unwrap_near(near, tile_count, spans)
        square[...] = jnp.zeros_like(square)
        rows = near.shape[0] // 9
        kept = 3 * tile_count
        for brick in range(9):
            near_ref[brick * kept : (brick + 1) * kept, :] = near[
                brick * rows : brick * rows + kept, :
            ]

    tile = first_tile + pl.program_id(0)
    quantities = near.shape[0] // 9 // tile_count
    widen_own(near, 4, tile_count, tile, square, wide)
    origin = wide[2 * TILE : 2 * TILE + 1, 0:1]
    pick_rows(picked, near, lists_ref, tile, tile_count, quantities, origin, spans[2])

    @pl.loop(0, TILE // PAIR_ROWS)
    def _(part):
        start = part * PAIR_ROWS
        for group in range(PAIR_ROWS // GROUP):
            own = [wide[wide_rows(start, group, dim), :] for dim in range(4)]
            own_damp = -thole_a * own[3]
            sums = [jnp.zeros((GROUP, TILE), jnp.float32) for _ in range(3 * RHS)]
            itself = (
                lax.broadcasted_iota(jnp.int32, (GROUP, TILE), 0) + (start + group * GROUP)
            ) == lax.broadcasted_iota(jnp.int32, (GROUP, TILE), 1)
            for entry in range(lists_ref.shape[1]):
                first = entry * quantities * GROUP
                rows = [
                    picked[first + quantity * GROUP : first + (quantity + 1) * GROUP, :]
                    for quantity in range(quantities)
                ]
                apart = [rows[dim] - own[dim] for dim in range(3)]
                square_dist = apart[0] * apart[0] + apart[1] * apart[1] + apart[2] * apart[2]
                if entry == 0:
                    square_dist = jnp.where(itself, 1.0, square_dist)
                first_term, second_term = pair_terms(square_dist, own_damp * rows[3])
                if entry == 0:
                    first_term = jnp.where(itself, 0.0, first_term)
                    second_term = jnp.where(itself, 0.0, second_term)
                place = wide_rows(start, group, entry)
                first_ref[place, :] = first_term
                second_ref[place, :] = second_term
                add_field(sums, first_term, second_term, apart, rows[4:])
            for index, value in enumerate(sums):
                sums_ref[wide_rows(start, group, index), :] = value

    finish_sums(field_ref, sums_ref)


def pair_second_body(
    tile_count,
    spans,
    lists_ref,
    near,
    up_ref,
    stack_ref,
    down_ref,
    first_ref,
    second_ref,
    field_ref,
    near_moment,
    picked,
    picked_moment,
    square,
    wide,
    sums_ref,
):
    @pl.when(pl.program_id(0) == 0)
    def _():
        fill_near(near_moment, up_ref, stack_ref, down_ref)
        square[...] = jnp.zeros_like(square)

    tile = pl.program_id(0)
    widen_own(near, 3, tile_count, tile, square, wide)
    origin = wide[2 * TILE : 2 * TILE + 1, 0:1]
    pick_rows(picked, near, lists_ref, tile, tile_count, 3, origin, spans[2])
    pick_rows(picked_moment, near_moment, lists_ref, tile, tile_count, 3 * RHS, None, None)

    @pl.loop(0, TILE // PAIR_ROWS)
    def _(part):
        start = part * PAIR_ROWS
        for group in range(PAIR_ROWS // GROUP):
            own = [wide[wide_rows(start, group, dim), :] for dim in range(3)]
            sums = [jnp.zeros((GROUP, TILE), jnp.float32) for _ in range(3 * RHS)]
            for entry in range(lists_ref.shape[1]):
                first = entry * 3 * GROUP
                apart = [
                    picked[first + dim * GROUP : first + (dim + 1) * GROUP, :] - own[dim]
                    for dim in range(3)
                ]
                first = first * RHS
                moments = [
                    picked_moment[first + index * GROUP : first + (index + 1) * GROUP, :]
                    for index in range(3 * RHS)
                ]
                place = wide_rows(start, group, entry)
                add_field(sums, first_ref[place, :], second_ref[place, :], apart, moments)
            for index, value in enumerate(sums):
                sums_ref[wide_rows(start, group, index), :] = value

    finish_sums(field_ref, sums_ref)


def shift(source, axis, step):
    count = lax.axis_size(axis)
    return lax.ppermute(source, axis, [(i, (i + step) % count) for i in range(count)])


def both_ways(source, axis):
    return shift(source, axis, 1), source, shift(source, axis, -1)


def whole(shape):
    return pl.BlockSpec(shape, lambda *_: (0,) * len(shape))


def anywhere():
    return pl.BlockSpec(memory_space=pl.ANY)


def join(message, payload):
    left, _, right = both_ways(payload, "col")
    message, left, right = lax.optimization_barrier((message, left, right))
    return message, both_ways(jnp.concatenate([left, payload, right], axis=0), "row")


class Fetched:
    def __init__(self, source, scratch, semaphore):
        self.copy = pltpu.make_async_copy(source, scratch, semaphore)
        self.copy.start()
        self.scratch = scratch
        self.shape = scratch.shape
        self.waiting = True

    def wait(self):
        if self.waiting:
            self.copy.wait()
            self.waiting = False

    def __getitem__(self, index):
        self.wait()
        return self.scratch[index]


def call(body, outs, *operands, after=(), own_block=None):
    fetched = [
        pltpu.VMEM(operand.shape[1:] if index == own_block else operand.shape, operand.dtype)
        for index, operand in enumerate(operands)
    ]
    count = len(operands)

    def run(*refs):
        refs = refs[len(after) :]
        sources, refs = refs[:count], refs[count:]
        results, refs = refs[: len(outs)], refs[len(outs) :]
        targets, written, semaphore = refs[:count], refs[count:-1], refs[-1]
        inputs = []
        for index, source in enumerate(sources):
            if index == own_block:
                place = lax.axis_index("row") * lax.axis_size("col") + lax.axis_index("col")
                source = source.at[place]
            inputs.append(Fetched(source, targets[index], semaphore.at[index]))
        body(*inputs, *written)
        for operand in inputs:
            operand.wait()
        copies = [
            pltpu.make_async_copy(value, result, semaphore.at[count + index])
            for index, (value, result) in enumerate(zip(written, results))
        ]
        for copy in copies:
            copy.start()
        for copy in copies:
            copy.wait()

    return pl.pallas_call(
        run,
        in_specs=[anywhere()] * (len(after) + count),
        out_specs=[anywhere()] * len(outs),
        out_shape=[jax.ShapeDtypeStruct(shape, dtype) for shape, dtype in outs],
        scratch_shapes=fetched
        + [pltpu.VMEM(shape, dtype) for shape, dtype in outs]
        + [pltpu.SemaphoreType.DMA((count + len(outs),))],
        compiler_params=pltpu.CompilerParams(vmem_limit_bytes=VMEM_LIMIT),
        cost_estimate=pl.CostEstimate(
            flops=200_000_000, bytes_accessed=4 << 20, transcendentals=0
        ),
    )(*after, *operands)


def final_call(body, outs, *operands):
    return pl.pallas_call(
        body,
        grid=(1,),
        in_specs=[whole(operand.shape) for operand in operands],
        out_specs=[whole(shape) for shape, _ in outs],
        out_shape=[jax.ShapeDtypeStruct(shape, dtype) for shape, dtype in outs],
        compiler_params=pltpu.CompilerParams(vmem_limit_bytes=SMALL_VMEM_LIMIT),
    )(*operands)


def pair_call(body, outs, kept, first_tile, last_tile, blocked, scratch, lists, *operands, after=()):
    tiles = lists.shape[0]

    def block(operand):
        rows = operand.shape[0] // tiles
        return pl.BlockSpec((rows, operand.shape[1]), lambda i, s: (first_tile + i, 0))

    out_shape = [jax.ShapeDtypeStruct(shape, jnp.float32) for shape in outs + kept]
    plain = len(operands) - blocked
    aliases = {}
    if first_tile > 0:
        first = 1 + len(operands) + len(after) - len(outs)
        aliases = {first + index: index for index in range(len(outs))}
    return pl.pallas_call(
        body,
        out_shape=out_shape,
        grid_spec=pltpu.PrefetchScalarGridSpec(
            num_scalar_prefetch=1,
            grid=(last_tile - first_tile,),
            in_specs=[whole(operand.shape) for operand in operands[:plain]]
            + [block(operand) for operand in operands[plain:]]
            + [anywhere()] * len(after),
            out_specs=[block(shape) for shape in out_shape[: len(outs)]]
            + [whole(shape) for shape in kept],
            scratch_shapes=[pltpu.VMEM(shape, jnp.float32) for shape in scratch],
        ),
        input_output_aliases=aliases,
        compiler_params=pltpu.CompilerParams(vmem_limit_bytes=VMEM_LIMIT),
        cost_estimate=pl.CostEstimate(
            flops=80_000_000, bytes_accessed=8 << 20, transcendentals=1 << 21
        ),
    )(lists, *operands, *after)


def exchange(message, devices):
    shape = message.shape
    sent = message.reshape(devices, 1, -1)
    return lax.all_to_all(sent, ("row", "col"), split_axis=0, concat_axis=0, tiled=True).reshape(
        shape
    )


def slab_local(field_rhs, positions, polar, grid_base, tile_lists):
    rows_count = lax.axis_size("row")
    cols_count = lax.axis_size("col")
    counts = (rows_count, cols_count)
    devices = rows_count * cols_count
    lengths = (CX * rows_count, CY * cols_count, KZ)
    spans = tuple(float(length) for length in lengths)
    atoms = polar.shape[-1]
    tile_count = atoms // TILE
    listed = tile_lists.shape[-1]
    tables = slab_tables(rows_count, cols_count)
    f32 = jnp.float32
    rhs = jnp.swapaxes(field_rhs[0, 0], 0, 1)
    place = jnp.swapaxes(positions[0], 0, 1)
    base = jnp.swapaxes(grid_base[0], 0, 1)
    polar = polar.reshape(1, atoms)
    lists = tile_lists[0, 0]
    quantities = 4 + 3 * RHS
    brick_rows = quantities * tile_count
    moment_rows = 3 * RHS * tile_count
    message_shape = (devices * X_PAD, KZ // devices * RHS * Y_PAD)
    last_shape = (devices * (X_PAD + 1), message_shape[1])
    row_shape = (3 * RHS, atoms)
    square = (TILE, TILE)
    wide = (4 * TILE, TILE)
    sums = (3 * RHS * TILE, TILE)

    start, payload = call(pack_body, [(row_shape, f32), ((brick_rows, TILE), f32)], rhs, place, polar)

    def setup(*refs):
        setup_body(lengths, devices, *refs)

    message, splines, depth_high, depth_low = call(
        setup,
        [
            (message_shape, f32),
            ((2 * SLOT_ROWS + 2 * Y_PAD, atoms), f32),
            ((KZ, 2 * atoms), jnp.bfloat16),
            ((KZ, 2 * atoms), jnp.bfloat16),
        ],
        place,
        base,
        start,
        *[jnp.asarray(table) for table in tables["along_z"]],
    )
    constants = (
        jnp.asarray(tables["kernel"]),
        jnp.asarray(tables["forward_x"]),
        jnp.asarray(tables["backward_x"]),
        *[jnp.asarray(table) for table in tables["block"]],
    )
    message, near = join(message, payload)
    arrived = exchange(message, devices)

    def pair_first(first_tile, last_tile, *after):
        def body(*refs):
            pair_first_body(first_tile, tile_count, spans, *refs)

        return pair_call(
            body,
            [(tile_count * listed * TILE, TILE)] * 2 + [(tile_count * GROUP, TILE)],
            [(9 * 3 * tile_count, TILE)],
            first_tile,
            last_tile,
            0,
            [(9 * brick_rows, TILE), (listed * quantities * GROUP, TILE), square, wide, sums],
            lists,
            *near,
            after=after,
        )

    early = pair_first(0, EARLY_TILES, message)

    def middle_first(*refs):
        middle_first_body(counts, *refs)

    mixed, wave = call(
        middle_first,
        [(message_shape, f32), (tables["kernel"].shape[1:], f32)],
        arrived,
        *constants,
        after=(early[2],),
        own_block=1,
    )
    returned = exchange(mixed, devices)
    first_term, second_term, direct, near = pair_first(EARLY_TILES, tile_count, wave, *early[:3])

    def sample(*refs):
        sample_body(devices, *refs)

    image, second, moments = call(
        sample,
        [(row_shape, f32), (row_shape, f32), ((moment_rows, TILE), f32)],
        returned,
        splines,
        depth_high,
        depth_low,
        start,
        direct,
        polar,
    )

    def spread(*refs):
        spread_body(devices, *refs)

    (message,) = call(spread, [(message_shape, f32)], splines, depth_high, depth_low, second)
    message, near_moments = join(message, moments)
    arrived = exchange(message, devices)

    def pair_second(*refs):
        pair_second_body(tile_count, spans, *refs)

    (direct,) = pair_call(
        pair_second,
        [(tile_count * GROUP, TILE)],
        [],
        0,
        tile_count,
        2,
        [
            (9 * moment_rows, TILE),
            (listed * 3 * GROUP, TILE),
            (listed * 3 * RHS * GROUP, TILE),
            square,
            wide,
            sums,
        ],
        lists,
        near,
        *near_moments,
        first_term,
        second_term,
    )

    def middle_second(*refs):
        middle_second_body(counts, *refs)

    (mixed,) = call(
        middle_second,
        [(last_shape, f32)],
        arrived,
        *constants,
        wave,
        rhs,
        start,
        image,
        second,
        direct,
        polar,
        own_block=1,
    )
    returned = exchange(mixed, devices)

    def final(*refs):
        final_body(devices, *refs)

    outs = final_call(
        final,
        [(rhs.shape, f32), (rhs.shape, f32)],
        returned,
        splines,
        depth_high,
        depth_low,
        rhs,
        start,
        image,
        second,
        direct,
        polar,
    )
    return tuple(jnp.swapaxes(out, 0, 1)[None, None] for out in outs)


def solution(mesh):
    placed = (
        P("row", "col", None, None, None),
        P("row", "col", None, None),
        P("row", "col", None),
        P("row", "col", None, None),
        P("row", "col", None, None),
    )
    devices = mesh.shape["row"] * mesh.shape["col"]
    return jax.shard_map(
        slab_local if KZ % devices == 0 else pencil_local,
        mesh=mesh,
        in_specs=placed,
        out_specs=(P("row", "col", None, None, None), P("row", "col", None, None, None)),
        check_vma=False,
    )
```

profile of v0, /device:TPU:0, one launch (start us, length us, event | category | flops | bytes accessed | tf_op | source)
XLA Modules:
  0.0 100.6 jit_solution(11231702574091504776)
XLA Ops:
  0.6 1.4 %shard_map.131 = (f32[6,512]{1,0:T(8,128)}, f32[40,128]{1,0:T(8,128)}) custom-call(f32[3,2,512]{2,1,0:T(2,128)} %bitcast.22, f32[3,1,512]{2,1,0:T(1,128)} %bitcast.41, f32[1,512]{1,0:T(1,128)} %bitcast.25), custom_call_target="tpu_custom_call" | custom-call | flops 200000000 | bytes 4194304 | tf_op jit(solution)/shard_map/pallas_call | solution.py:1137
  2.0 3.0 %collective-permute-start = (f32[40,128]{1,0:T(8,128)}, f32[40,128]{1,0:T(8,128)S(1)}, u32[]{:S(2)}, u32[]{:S(2)}) collective-permute-start(f32[40,128]{1,0:T(8,128)} %get-tuple-element.33), channel_id=1, source_target_pairs={{0,1},{1,2},{2,3},{3,4},{4,5},{5,6},{6,7},{7,0},{8,9},{9,10},{10,1... | collective-permute-start | bytes 61448 | tf_op jit(solution)/shard_map/ppermute | solution.py:1068
  5.1 3.1 %collective-permute-start.1 = (f32[40,128]{1,0:T(8,128)}, f32[40,128]{1,0:T(8,128)S(1)}, u32[]{:S(2)}, u32[]{:S(2)}) collective-permute-start(f32[40,128]{1,0:T(8,128)} %get-tuple-element.33), channel_id=1, source_target_pairs={{0,7},{1,0},{2,1},{3,2},{4,3},{5,4},{6,5},{7,6},{8,15},{9,8},{10,9... | collective-permute-start | bytes 61448 | tf_op jit(solution)/shard_map/ppermute | solution.py:1068
  8.2 5.0 %shard_map.132 = (f32[384,128]{1,0:T(8,128)}, f32[48,512]{1,0:T(8,128)}, bf16[256,1024]{1,0:T(8,128)(2,1)}, bf16[256,1024]{1,0:T(8,128)(2,1)}) custom-call(f32[3,1,512]{2,1,0:T(1,128)} %bitcast.42, s32[3,1,512]{2,1,0:T(1,128)} %bitcast.43, f32[6,512]{1,0:T(8,128)} %get-tuple-element.28.refs_2_.refs_4_.refs_8_.refs_5_, ...), custom_call_target="tpu_custom_call" | custom-call | flops 200000000 | bytes 4194304 | tf_op jit(solution)/shard_map/pallas_call | solution.py:1137
  13.2 3.3 %all-to-all-start = ((f32[32,1,1536]{2,1,0:T(1,128)}), f32[32,1,1536]{2,1,0:T(1,128)S(1)}, u32[]{:S(2)}, u32[]{:S(2)}) async-start(f32[32,1,1536]{2,1,0:T(1,128)} %bitcast.34), calls=%async_computation | async-start | bytes 393216 | tf_op jit(solution)/shard_map/all_to_all | solution.py:1200
  16.5 0.7 constant_dynamic-update-slice_fusion.1
  17.2 0.3 collective-permute-start.2
  17.4 1.5 %collective-permute-start.3 = (f32[120,128]{1,0:T(8,128)S(1)}, f32[120,128]{1,0:T(8,128)S(1)}, u32[]{:S(2)}, u32[]{:S(2)}) collective-permute-start(f32[120,128]{1,0:T(8,128)S(1)} %constant_dynamic-update-slice_fusion.refs_2_), channel_id=1, source_target_pairs={{0,24},{8,0},{16,8},{24,16},{1,25},{9,1},{17,9},{25,17},{2,26},{10... | collective-permute-start | bytes 184328 | tf_op jit(solution)/shard_map/ppermute | solution.py:1068
  18.9 2.4 %collective-permute-done.2.refs_1_ = f32[120,128]{1,0:T(8,128)S(1)} collective-permute-done((f32[120,128]{1,0:T(8,128)S(1)}, f32[120,128]{1,0:T(8,128)S(1)}, u32[]{:S(2)}, u32[]{:S(2)}) %collective-permute-start.2) | collective-permute-done | bytes 61472 | tf_op jit(solution)/shard_map/ppermute | solution.py:1068
  21.4 0.6 copy-done.14
  22.0 0.0 copy-done.15
  22.0 5.5 %shard_map.133 = (f32[6144,128]{1,0:T(8,128)}, f32[6144,128]{1,0:T(8,128)}, f32[32,128]{1,0:T(8,128)}, f32[108,128]{1,0:T(8,128)}) custom-call(s32[4,12]{1,0:T(4,128)} %bitcast.36, f32[120,128]{1,0:T(8,128)} %copy-done.14, f32[120,128]{1,0:T(8,128)} %copy-done.12, f32[120,128]{1,0:T(8,128)} %copy-done.15, f32[384,128]{1,0:T(8,128)} %get-tuple-element.36.refs_4_), custom_call_target="tpu_custom_call" | custom-call | flops 80000000 | bytes 8388608 | tf_op jit(solution)/shard_map/pallas_call | solution.py:1176
  27.5 0.7 copy-done.9
  28.2 3.1 %shard_map.134 = (f32[384,128]{1,0:T(8,128)}, f32[64,256]{1,0:T(8,128)}) custom-call(f32[32,128]{1,0:T(8,128)} %get-tuple-element.37.refs_0_.refs_7_, f32[384,128]{1,0:T(8,128)} %bitcast.30, f32[32,64,256]{2,1,0:T(8,128)} %constant.16.clone.refs_2_.refs_1_, bf16[32,144]{1,0:T(8,128)(2,1)} %constant.17.clone.refs_3_.refs_2_, ...), custom_call_target="tpu_custom_call" | custom-call | flops 200000000 | bytes 4194304 | tf_op jit(solution)/shard_map/pallas_call | solution.py:1137
  31.3 6.2 %all-to-all-start.1 = ((f32[32,1,1536]{2,1,0:T(1,128)}), f32[32,1,1536]{2,1,0:T(1,128)S(1)}, u32[]{:S(2)}, u32[]{:S(2)}) async-start(f32[32,1,1536]{2,1,0:T(1,128)} %bitcast.35), calls=%async_computation.1 | async-start | bytes 393216 | tf_op jit(solution)/shard_map/all_to_all | solution.py:1200
  37.5 11.4 %shard_map.135 = (f32[6144,128]{1,0:T(8,128)}, f32[6144,128]{1,0:T(8,128)}, f32[32,128]{1,0:T(8,128)}, f32[108,128]{1,0:T(8,128)}) custom-call(s32[4,12]{1,0:T(4,128)} %bitcast.37, f32[120,128]{1,0:T(8,128)} %copy-done.14, f32[120,128]{1,0:T(8,128)} %copy-done.12, f32[120,128]{1,0:T(8,128)} %copy-done.15, ...), custom_call_target="tpu_custom_call", output_to_operand_aliasing={{0}: (5, {}), {1}: (6, {}), {2}: (7, {})} | custom-call | flops 80000000 | bytes 8388608 | tf_op jit(solution)/shard_map/pallas_call | solution.py:1176
  48.9 0.7 copy-done.10
  49.5 3.0 %shard_map.136 = (f32[6,512]{1,0:T(8,128)}, f32[6,512]{1,0:T(8,128)}, f32[24,128]{1,0:T(8,128)}) custom-call(f32[384,128]{1,0:T(8,128)} %bitcast.32, f32[48,512]{1,0:T(8,128)} %get-tuple-element.29.refs_1_.refs_0_, bf16[256,1024]{1,0:T(8,128)(2,1)} %get-tuple-element.30.refs_2_.refs_1_, bf16[256,1024]{1,0:T(8,128)(2,1)} %get-tuple-element.31.refs_3_.refs_2_, ...), custom_call_target="tpu_custom_call" | custom-call | flops 200000000 | bytes 4194304 | tf_op jit(solution)/shard_map/pallas_call | solution.py:1137
  52.6 1.8 %collective-permute-start.4 = (f32[24,128]{1,0:T(8,128)}, f32[24,128]{1,0:T(8,128)S(1)}, u32[]{:S(2)}, u32[]{:S(2)}) collective-permute-start(f32[24,128]{1,0:T(8,128)} %get-tuple-element.44), channel_id=1, source_target_pairs={{0,1},{1,2},{2,3},{3,4},{4,5},{5,6},{6,7},{7,0},{8,9},{9,10},{10,1... | collective-permute-start | bytes 36872 | tf_op jit(solution)/shard_map/ppermute | solution.py:1068
  54.4 2.9 %collective-permute-start.5 = (f32[24,128]{1,0:T(8,128)}, f32[24,128]{1,0:T(8,128)S(1)}, u32[]{:S(2)}, u32[]{:S(2)}) collective-permute-start(f32[24,128]{1,0:T(8,128)} %get-tuple-element.44), channel_id=1, source_target_pairs={{0,7},{1,0},{2,1},{3,2},{4,3},{5,4},{6,5},{7,6},{8,15},{9,8},{10,9... | collective-permute-start | bytes 36872 | tf_op jit(solution)/shard_map/ppermute | solution.py:1068
  57.3 3.0 %shard_map.137 = f32[384,128]{1,0:T(8,128)} custom-call(f32[48,512]{1,0:T(8,128)} %get-tuple-element.29.refs_1_.refs_0_, bf16[256,1024]{1,0:T(8,128)(2,1)} %get-tuple-element.30.refs_2_.refs_1_, bf16[256,1024]{1,0:T(8,128)(2,1)} %get-tuple-element.31.refs_3_.refs_2_, f32[6,512]{1,0:T(8,128)} %get-tuple-element.43.refs_3_.refs_10_.refs_7_), custom_call_target="tpu_custom_call" | custom-call | flops 200000000 | bytes 4194304 | tf_op jit(solution)/shard_map/pallas_call | solution.py:1137
  60.4 5.1 %all-to-all-start.2 = ((f32[32,1,1536]{2,1,0:T(1,128)}), f32[32,1,1536]{2,1,0:T(1,128)S(1)}, u32[]{:S(2)}, u32[]{:S(2)}) async-start(f32[32,1,1536]{2,1,0:T(1,128)} %bitcast.31), calls=%async_computation.2 | async-start | bytes 393216 | tf_op jit(solution)/shard_map/all_to_all | solution.py:1200
  65.5 0.7 constant_dynamic-update-slice_fusion.4
  66.2 0.3 collective-permute-start.6
  66.5 1.5 %collective-permute-start.7 = (f32[72,128]{1,0:T(8,128)S(1)}, f32[72,128]{1,0:T(8,128)S(1)}, u32[]{:S(2)}, u32[]{:S(2)}) collective-permute-start(f32[72,128]{1,0:T(8,128)S(1)} %constant_dynamic-update-slice_fusion.3.refs_3_), channel_id=1, source_target_pairs={{0,24},{8,0},{16,8},{24,16},{1,25},{9,1},{17,9},{25,17},{2,26},{10... | collective-permute-start | bytes 110600 | tf_op jit(solution)/shard_map/ppermute | solution.py:1068
  68.0 1.9 %collective-permute-done.6.refs_2_ = f32[72,128]{1,0:T(8,128)S(1)} collective-permute-done((f32[72,128]{1,0:T(8,128)S(1)}, f32[72,128]{1,0:T(8,128)S(1)}, u32[]{:S(2)}, u32[]{:S(2)}) %collective-permute-start.6) | collective-permute-done | bytes 36896 | tf_op jit(solution)/shard_map/ppermute | solution.py:1068
  69.9 0.6 copy-done.16
  70.5 8.8 %shard_map.138.refs_11_.refs_8_ = f32[32,128]{1,0:T(8,128)} custom-call(s32[4,12]{1,0:T(4,128)} %bitcast.38, f32[108,128]{1,0:T(8,128)} %get-tuple-element.47.refs_1_, f32[72,128]{1,0:T(8,128)} %copy-done.16, f32[72,128]{1,0:T(8,128)} %copy-done.13, f32[72,128]{1,0:T(8,128)} %copy-done.17, f32[6144,128]{1,0:T(8,128)} %get-tuple-element.50.refs_5_, ...), custom_call_target="tpu_custom_call" | custom-call | flops 80000000 | bytes 8388608 | tf_op jit(solution)/shard_map/pallas_call | solution.py:1176
  79.4 0.7 copy-done.11
  80.1 3.4 %shard_map.139 = f32[416,128]{1,0:T(8,128)} custom-call(f32[384,128]{1,0:T(8,128)} %bitcast.33, f32[32,64,256]{2,1,0:T(8,128)} %constant.16.clone.refs_2_.refs_1_, bf16[32,144]{1,0:T(8,128)(2,1)} %constant.17.clone.refs_3_.refs_2_, bf16[48,96]{1,0:T(8,128)(2,1)} %constant.18.clone.refs_4_.refs_3_, bf16[512,256]{1,0:T(8,128)(2,1)} %constant.19.clone.refs_5_.refs_4_, ...), custom_call_target="tpu_custom_call" | custom-call | flops 200000000 | bytes 4194304 | tf_op jit(solution)/shard_map/pallas_call | solution.py:1137
  83.6 15.4 %all_to_all.20 = f32[32,1,1664]{2,1,0:T(1,128)S(1)} all-to-all(f32[32,1,1664]{2,1,0:T(1,128)} %bitcast.29), channel_id=1, replica_groups=mesh['row'=4,'col'=8] {'row','col'}, dimensions={0} | all-to-all | bytes 425984 | tf_op jit(solution)/shard_map/all_to_all | solution.py:1200
  99.0 1.5 %shard_map.140 = (f32[3,2,512]{2,1,0:T(2,128)}, f32[3,2,512]{2,1,0:T(2,128)}) custom-call(f32[416,128]{1,0:T(8,128)S(1)} %bitcast.21, f32[48,512]{1,0:T(8,128)S(1)} %copy-done.2, bf16[256,1024]{1,0:T(8,128)(2,1)S(1)} %copy-done, bf16[256,1024]{1,0:T(8,128)(2,1)S(1)} %copy-done.1, f32[3,2,512]{2,1,0:T(2,128)S(1)} %bitcast.24, f32[6,512]{1,0:T(8,128)S(1)} %copy-done.3, ...), custom_call_target="tpu_custom_call" | custom-call | tf_op jit(solution)/shard_map/pallas_call | solution.py:1153
  (43 shorter events, 0.1 us)
Async XLA Ops:
  2.0 11.1 %collective-permute-start = (f32[40,128]{1,0:T(8,128)}, f32[40,128]{1,0:T(8,128)S(1)}, u32[]{:S(2)}, u32[]{:S(2)}) collective-permute-start(f32[40,128]{1,0:T(8,128)} %get-tuple-element.33), channel_id=1, source_target_pairs={{0,1},{1,2},{2,3},{3,4},{4,5},{5,6},{6,7},{7,0},{8,9},{9,10},{10,1... | collective-permute-start | bytes 61448 | tf_op jit(solution)/shard_map/ppermute | solution.py:1068
  5.1 8.1 %collective-permute-start.1 = (f32[40,128]{1,0:T(8,128)}, f32[40,128]{1,0:T(8,128)S(1)}, u32[]{:S(2)}, u32[]{:S(2)}) collective-permute-start(f32[40,128]{1,0:T(8,128)} %get-tuple-element.33), channel_id=1, source_target_pairs={{0,7},{1,0},{2,1},{3,2},{4,3},{5,4},{6,5},{7,6},{8,15},{9,8},{10,9... | collective-permute-start | bytes 61448 | tf_op jit(solution)/shard_map/ppermute | solution.py:1068
  13.2 14.3 %all-to-all-start = ((f32[32,1,1536]{2,1,0:T(1,128)}), f32[32,1,1536]{2,1,0:T(1,128)S(1)}, u32[]{:S(2)}, u32[]{:S(2)}) async-start(f32[32,1,1536]{2,1,0:T(1,128)} %bitcast.34), calls=%async_computation | async-start | bytes 393216 | tf_op jit(solution)/shard_map/all_to_all | solution.py:1200
  17.2 4.2 %copy-start.12 = (f32[120,128]{1,0:T(8,128)}, f32[120,128]{1,0:T(8,128)S(1)}, u32[]{:S(2)}) copy-start(f32[120,128]{1,0:T(8,128)S(1)} %constant_dynamic-update-slice_fusion.refs_2_) | copy-start | bytes 184324
  17.2 4.2 %collective-permute-start.2 = (f32[120,128]{1,0:T(8,128)S(1)}, f32[120,128]{1,0:T(8,128)S(1)}, u32[]{:S(2)}, u32[]{:S(2)}) collective-permute-start(f32[120,128]{1,0:T(8,128)S(1)} %constant_dynamic-update-slice_fusion.refs_2_), channel_id=1, source_target_pairs={{0,8},{8,16},{16,24},{24,0},{1,9},{9,17},{17,25},{25,1},{2,10},{10... | collective-permute-start | bytes 184328 | tf_op jit(solution)/shard_map/ppermute | solution.py:1068
  17.4 3.9 %collective-permute-start.3 = (f32[120,128]{1,0:T(8,128)S(1)}, f32[120,128]{1,0:T(8,128)S(1)}, u32[]{:S(2)}, u32[]{:S(2)}) collective-permute-start(f32[120,128]{1,0:T(8,128)S(1)} %constant_dynamic-update-slice_fusion.refs_2_), channel_id=1, source_target_pairs={{0,24},{8,0},{16,8},{24,16},{1,25},{9,1},{17,9},{25,17},{2,26},{10... | collective-permute-start | bytes 184328 | tf_op jit(solution)/shard_map/ppermute | solution.py:1068
  21.4 0.6 copy-start.14
  21.4 0.6 copy-start.15
  27.5 0.7 copy-start.9
  31.3 17.5 %all-to-all-start.1 = ((f32[32,1,1536]{2,1,0:T(1,128)}), f32[32,1,1536]{2,1,0:T(1,128)S(1)}, u32[]{:S(2)}, u32[]{:S(2)}) async-start(f32[32,1,1536]{2,1,0:T(1,128)} %bitcast.35), calls=%async_computation.1 | async-start | bytes 393216 | tf_op jit(solution)/shard_map/all_to_all | solution.py:1200
  48.8 0.7 copy-start.10
  52.6 7.8 %collective-permute-start.4 = (f32[24,128]{1,0:T(8,128)}, f32[24,128]{1,0:T(8,128)S(1)}, u32[]{:S(2)}, u32[]{:S(2)}) collective-permute-start(f32[24,128]{1,0:T(8,128)} %get-tuple-element.44), channel_id=1, source_target_pairs={{0,1},{1,2},{2,3},{3,4},{4,5},{5,6},{6,7},{7,0},{8,9},{9,10},{10,1... | collective-permute-start | bytes 36872 | tf_op jit(solution)/shard_map/ppermute | solution.py:1068
  54.4 6.0 %collective-permute-start.5 = (f32[24,128]{1,0:T(8,128)}, f32[24,128]{1,0:T(8,128)S(1)}, u32[]{:S(2)}, u32[]{:S(2)}) collective-permute-start(f32[24,128]{1,0:T(8,128)} %get-tuple-element.44), channel_id=1, source_target_pairs={{0,7},{1,0},{2,1},{3,2},{4,3},{5,4},{6,5},{7,6},{8,15},{9,8},{10,9... | collective-permute-start | bytes 36872 | tf_op jit(solution)/shard_map/ppermute | solution.py:1068
  60.4 19.0 %all-to-all-start.2 = ((f32[32,1,1536]{2,1,0:T(1,128)}), f32[32,1,1536]{2,1,0:T(1,128)S(1)}, u32[]{:S(2)}, u32[]{:S(2)}) async-start(f32[32,1,1536]{2,1,0:T(1,128)} %bitcast.31), calls=%async_computation.2 | async-start | bytes 393216 | tf_op jit(solution)/shard_map/all_to_all | solution.py:1200
  66.2 3.7 %copy-start.13 = (f32[72,128]{1,0:T(8,128)}, f32[72,128]{1,0:T(8,128)S(1)}, u32[]{:S(2)}) copy-start(f32[72,128]{1,0:T(8,128)S(1)} %constant_dynamic-update-slice_fusion.3.refs_3_) | copy-start | bytes 110596
  66.2 3.6 %collective-permute-start.6 = (f32[72,128]{1,0:T(8,128)S(1)}, f32[72,128]{1,0:T(8,128)S(1)}, u32[]{:S(2)}, u32[]{:S(2)}) collective-permute-start(f32[72,128]{1,0:T(8,128)S(1)} %constant_dynamic-update-slice_fusion.3.refs_3_), channel_id=1, source_target_pairs={{0,8},{8,16},{16,24},{24,0},{1,9},{9,17},{17,25},{25,1},{2,10},{10... | collective-permute-start | bytes 110600 | tf_op jit(solution)/shard_map/ppermute | solution.py:1068
  66.5 3.4 %collective-permute-start.7 = (f32[72,128]{1,0:T(8,128)S(1)}, f32[72,128]{1,0:T(8,128)S(1)}, u32[]{:S(2)}, u32[]{:S(2)}) collective-permute-start(f32[72,128]{1,0:T(8,128)S(1)} %constant_dynamic-update-slice_fusion.3.refs_3_), channel_id=1, source_target_pairs={{0,24},{8,0},{16,8},{24,16},{1,25},{9,1},{17,9},{25,17},{2,26},{10... | collective-permute-start | bytes 110600 | tf_op jit(solution)/shard_map/ppermute | solution.py:1068
  69.9 0.6 copy-start.16
  69.9 0.6 copy-start.17
  79.3 19.6 %copy-start = (bf16[256,1024]{1,0:T(8,128)(2,1)S(1)}, bf16[256,1024]{1,0:T(8,128)(2,1)}, u32[]{:S(2)}) copy-start(bf16[256,1024]{1,0:T(8,128)(2,1)} %get-tuple-element.30.refs_2_.refs_1_) | copy-start | bytes 1572868
  79.3 19.6 %copy-start.1 = (bf16[256,1024]{1,0:T(8,128)(2,1)S(1)}, bf16[256,1024]{1,0:T(8,128)(2,1)}, u32[]{:S(2)}) copy-start(bf16[256,1024]{1,0:T(8,128)(2,1)} %get-tuple-element.31.refs_3_.refs_2_) | copy-start | bytes 1572868
  79.3 19.6 %copy-start.2 = (f32[48,512]{1,0:T(8,128)S(1)}, f32[48,512]{1,0:T(8,128)}, u32[]{:S(2)}) copy-start(f32[48,512]{1,0:T(8,128)} %get-tuple-element.29.refs_1_.refs_0_) | copy-start | bytes 294916
  79.4 19.6 %copy-start.3 = (f32[6,512]{1,0:T(8,128)S(1)}, f32[6,512]{1,0:T(8,128)}, u32[]{:S(2)}) copy-start(f32[6,512]{1,0:T(8,128)} %get-tuple-element.28.refs_2_.refs_4_.refs_8_.refs_5_) | copy-start | bytes 36868
  79.4 19.6 %copy-start.4 = (f32[6,512]{1,0:T(8,128)S(1)}, f32[6,512]{1,0:T(8,128)}, u32[]{:S(2)}) copy-start(f32[6,512]{1,0:T(8,128)} %get-tuple-element.43.refs_3_.refs_10_.refs_7_) | copy-start | bytes 36868
  79.4 19.6 %copy-start.5 = (f32[32,128]{1,0:T(8,128)S(1)}, f32[32,128]{1,0:T(8,128)}, u32[]{:S(2)}) copy-start(f32[32,128]{1,0:T(8,128)} %shard_map.138.refs_11_.refs_8_) | copy-start | bytes 49156
  79.4 19.6 %copy-start.6 = (f32[6,512]{1,0:T(8,128)S(1)}, f32[6,512]{1,0:T(8,128)}, u32[]{:S(2)}) copy-start(f32[6,512]{1,0:T(8,128)} %get-tuple-element.46.refs_9_.refs_6_) | copy-start | bytes 36868
  79.4 19.6 %copy-start.7 = (f32[1,1,2,3,512]{4,2,3,1,0:T(2,128)S(1)}, f32[1,1,2,3,512]{4,2,3,1,0:T(2,128)}, u32[]{:S(2)}) copy-start(f32[1,1,2,3,512]{4,2,3,1,0:T(2,128)} %param.12) | copy-start | bytes 36868
  79.4 19.6 %copy-start.8 = (f32[1,1,512]{2,1,0:T(1,128)S(1)}, f32[1,1,512]{2,1,0:T(1,128)}, u32[]{:S(2)}) copy-start(f32[1,1,512]{2,1,0:T(1,128)} %param.14) | copy-start | bytes 6148
  79.4 0.7 copy-start.11
where the time goes:
time: 101 us
  Pallas kernels  46.2 us (46%)
  starting transfers between devices  28.9 us (29%)
  blocking collectives  15.4 us (15%)
  local copies, waits for them, and re-layouts  4.81 us (5%)
  waiting for transfers between devices  4.35 us (4%)
    pallas_call x3, Pallas kernels, pair_call(): pl.pallas_call(body, out_shape=out_shape, grid_spec=pltpu.PrefetchScalarG...  25.6 us
    pallas_call x6, Pallas kernels, call(): pl.pallas_call(run, in_specs=[anywhere()] * (len(after) + count), out_spe...  19 us
    all_to_all x1, blocking collectives, exchange(): lax.all_to_all(sent, ('row', 'col'), split_axis=0, concat_axis=0, tiled=T...  15.4 us
    all_to_all x3, starting transfers between devices, exchange(): lax.all_to_all(sent, ('row', 'col'), split_axis=0, concat_axis=0, tiled=T...  14.6 us
    ppermute x8, starting transfers between devices, shift(): lax.ppermute(source, axis, [(i, (i + step) % count) for i in range(count)])  14.4 us
    unnamed x40, local copies, waits for them, and re-layouts  4.8 us
    ppermute x8, waiting for transfers between devices, shift(): lax.ppermute(source, axis, [(i, (i + step) % count) for i in range(count)])  4.34 us
  transfers between devices with their start and end apart: 11, of which 2 were waited for; matrix products, arithmetic and copies ran while one was open for 1% of the time, Pallas kernels for 33%

commit v1 on v0

--- a/solution.py
+++ b/solution.py
@@ -868,27 +868,30 @@
             )
 
 
-def pick_rows(picked, near, lists_ref, tile, tile_count, quantities, origin, span):
+def pick_rows(picked, near, lists_ref, tile, place, tile_count, quantities, origin, span):
     rows = near.shape[0] // 9
+    place = place * lists_ref.shape[1] * quantities * GROUP
     for entry in range(lists_ref.shape[1]):
         base = near_base(lists_ref[tile, entry], rows)
         for quantity in range(quantities):
             values = near[pl.ds(base + quantity * tile_count, 1), :]
             if quantity == 2 and span is not None:
                 values = nearest(values, origin, span)
-            first = (entry * quantities + quantity) * GROUP
+            first = place + (entry * quantities + quantity) * GROUP
             picked[first : first + GROUP, :] = jnp.broadcast_to(values, (GROUP, TILE))
 
 
-def widen_own(near, quantities, tile_count, tile, square, wide):
+def widen_own(near, quantities, tile_count, tile, place, wide):
     offset = near.shape[0] // 9 * 4
+    rows = [
+        near[offset + quantity * tile_count + tile : offset + quantity * tile_count + tile + 1, :]
+        for quantity in range(quantities)
+    ]
+    spare = jnp.zeros((TILE - quantities, TILE), jnp.float32)
+    columns = jnp.transpose(jnp.concatenate(rows + [spare], axis=0))
     for quantity in range(quantities):
-        square[quantity : quantity + 1, :] = near[
-            pl.ds(offset + quantity * tile_count + tile, 1), :
-        ]
-    columns = jnp.transpose(square[...])
-    for quantity in range(quantities):
-        wide[quantity * TILE : (quantity + 1) * TILE, :] = jnp.broadcast_to(
+        first = (place * quantities + quantity) * TILE
+        wide[first : first + TILE, :] = jnp.broadcast_to(
             columns[:, quantity : quantity + 1], (TILE, TILE)
         )
 
@@ -903,13 +906,16 @@
             sums[index] = sums[index] + (weighted * apart[dim] - first_term * moment[dim])
 
 
-def finish_sums(field_ref, sums_ref):
+def finish_sums(field_ref, sums_ref, first_tile, place):
+    place = place * 3 * RHS
     lane = lax.broadcasted_iota(jnp.int32, (TILE, TILE), 1)
     merged = jnp.zeros((TILE, TILE), jnp.float32)
     for index in range(3 * RHS):
-        column = jnp.sum(sums_ref[index * TILE : (index + 1) * TILE, :], axis=1, keepdims=True)
+        first = (place + index) * TILE
+        column = jnp.sum(sums_ref[first : first + TILE, :], axis=1, keepdims=True)
         merged = jnp.where(lane == index, column, merged)
-    field_ref[...] = jnp.transpose(merged)[0:GROUP]
+    first = (first_tile + place // (3 * RHS)) * GROUP
+    field_ref[first : first + GROUP, :] = jnp.transpose(merged)[0:GROUP]
 
 
 def pair_rows(start, group):
@@ -947,6 +953,7 @@
 
 def pair_first_body(
     first_tile,
+    last_tile,
     tile_count,
     spans,
     lists_ref,
@@ -955,25 +962,34 @@
     down_ref,
     *others,
 ):
-    first_ref, second_ref, field_ref, near_ref, near, picked, square, wide, sums_ref = others[-9:]
-
-    @pl.when(pl.program_id(0) == 0)
+    first_ref, second_ref, field_ref, near_ref, near, picked, wide, sums_ref = others[-8:]
+    quantities = near.shape[0] // 9 // tile_count
+    step = pl.program_id(0)
+    entries = lists_ref.shape[1]
+
+    @pl.when(step == 0)
     def _():
         fill_near(near, up_ref, stack_ref, down_ref)
         unwrap_near(near, tile_count, spans)
-        square[...] = jnp.zeros_like(square)
         rows = near.shape[0] // 9
         kept = 3 * tile_count
         for brick in range(9):
             near_ref[brick * kept : (brick + 1) * kept, :] = near[
                 brick * rows : brick * rows + kept, :
             ]
-
-    tile = first_tile + pl.program_id(0)
-    quantities = near.shape[0] // 9 // tile_count
-    widen_own(near, 4, tile_count, tile, square, wide)
-    origin = wide[2 * TILE : 2 * TILE + 1, 0:1]
-    pick_rows(picked, near, lists_ref, tile, tile_count, quantities, origin, spans[2])
+        for place, tile in enumerate(range(first_tile, last_tile)):
+            widen_own(near, 4, tile_count, tile, place, wide)
+            own = near.shape[0] // 9 * 4 + 2 * tile_count + tile
+            origin = near[own : own + 1, 0:1]
+            pick_rows(
+                picked, near, lists_ref, tile, place, tile_count, quantities, origin, spans[2]
+            )
+        if first_tile > 0:
+            field_ref[0 : first_tile * GROUP, :] = others[0][...]
+
+    picked = picked.at[tile_rows(step, entries * quantities * GROUP), :]
+    wide = wide.at[tile_rows(step, 4 * TILE), :]
+    step_sums = sums_ref.at[tile_rows(step, 3 * RHS * TILE), :]
 
     @pl.loop(0, TILE // PAIR_ROWS)
     def _(part):
@@ -985,7 +1001,7 @@
             itself = (
                 lax.broadcasted_iota(jnp.int32, (GROUP, TILE), 0) + (start + group * GROUP)
             ) == lax.broadcasted_iota(jnp.int32, (GROUP, TILE), 1)
-            for entry in range(lists_ref.shape[1]):
+            for entry in range(entries):
                 first = entry * quantities * GROUP
                 rows = [
                     picked[first + quantity * GROUP : first + (quantity + 1) * GROUP, :]
@@ -1004,9 +1020,16 @@
                 second_ref[place, :] = second_term
                 add_field(sums, first_term, second_term, apart, rows[4:])
             for index, value in enumerate(sums):
-                sums_ref[wide_rows(start, group, index), :] = value
-
-    finish_sums(field_ref, sums_ref)
+                step_sums[wide_rows(start, group, index), :] = value
+
+    @pl.when(step == last_tile - first_tile - 1)
+    def _():
+        for place in range(last_tile - first_tile):
+            finish_sums(field_ref, sums_ref, first_tile, place)
+
+
+def tile_rows(step, rows):
+    return pl.ds(pl.multiple_of(step * rows, GROUP), rows)
 
 
 def pair_second_body(
@@ -1023,20 +1046,28 @@
     near_moment,
     picked,
     picked_moment,
-    square,
     wide,
     sums_ref,
 ):
-    @pl.when(pl.program_id(0) == 0)
+    step = pl.program_id(0)
+    entries = lists_ref.shape[1]
+
+    @pl.when(step == 0)
     def _():
         fill_near(near_moment, up_ref, stack_ref, down_ref)
-        square[...] = jnp.zeros_like(square)
-
-    tile = pl.program_id(0)
-    widen_own(near, 3, tile_count, tile, square, wide)
-    origin = wide[2 * TILE : 2 * TILE + 1, 0:1]
-    pick_rows(picked, near, lists_ref, tile, tile_count, 3, origin, spans[2])
-    pick_rows(picked_moment, near_moment, lists_ref, tile, tile_count, 3 * RHS, None, None)
+        for tile in range(tile_count):
+            widen_own(near, 3, tile_count, tile, tile, wide)
+            own = near.shape[0] // 9 * 4 + 2 * tile_count + tile
+            origin = near[own : own + 1, 0:1]
+            pick_rows(picked, near, lists_ref, tile, tile, tile_count, 3, origin, spans[2])
+            pick_rows(
+                picked_moment, near_moment, lists_ref, tile, tile, tile_count, 3 * RHS, None, None
+            )
+
+    picked = picked.at[tile_rows(step, entries * 3 * GROUP), :]
+    picked_moment = picked_moment.at[tile_rows(step, entries * 3 * RHS * GROUP), :]
+    wide = wide.at[tile_rows(step, 3 * TILE), :]
+    step_sums = sums_ref.at[tile_rows(step, 3 * RHS * TILE), :]
 
     @pl.loop(0, TILE // PAIR_ROWS)
     def _(part):
@@ -1044,7 +1075,7 @@
         for group in range(PAIR_ROWS // GROUP):
             own = [wide[wide_rows(start, group, dim), :] for dim in range(3)]
             sums = [jnp.zeros((GROUP, TILE), jnp.float32) for _ in range(3 * RHS)]
-            for entry in range(lists_ref.shape[1]):
+            for entry in range(entries):
                 first = entry * 3 * GROUP
                 apart = [
                     picked[first + dim * GROUP : first + (dim + 1) * GROUP, :] - own[dim]
@@ -1058,9 +1089,12 @@
                 place = wide_rows(start, group, entry)
                 add_field(sums, first_ref[place, :], second_ref[place, :], apart, moments)
             for index, value in enumerate(sums):
-                sums_ref[wide_rows(start, group, index), :] = value
-
-    finish_sums(field_ref, sums_ref)
+                step_sums[wide_rows(start, group, index), :] = value
+
+    @pl.when(step == tile_count - 1)
+    def _():
+        for place in range(tile_count):
+            finish_sums(field_ref, sums_ref, 0, place)
 
 
 def shift(source, axis, step):
@@ -1080,8 +1114,20 @@
     return pl.BlockSpec(memory_space=pl.ANY)
 
 
+def pairwise(source, axis):
+    count = lax.axis_size(axis)
+    first = lax.ppermute(source, axis, [(i, i ^ 1) for i in range(count)])
+    second = lax.ppermute(
+        source, axis, [(i, (i + 1 if i % 2 else i - 1) % count) for i in range(count)]
+    )
+    return first, second
+
+
 def join(message, payload):
-    left, _, right = both_ways(payload, "col")
+    first, second = pairwise(payload, "col")
+    even = lax.rem(lax.axis_index("col"), 2) == 0
+    left = jnp.where(even, second, first)
+    right = jnp.where(even, first, second)
     message, left, right = lax.optimization_barrier((message, left, right))
     return message, both_ways(jnp.concatenate([left, payload, right], axis=0), "row")
 
@@ -1225,9 +1271,6 @@
     message_shape = (devices * X_PAD, KZ // devices * RHS * Y_PAD)
     last_shape = (devices * (X_PAD + 1), message_shape[1])
     row_shape = (3 * RHS, atoms)
-    square = (TILE, TILE)
-    wide = (4 * TILE, TILE)
-    sums = (3 * RHS * TILE, TILE)
 
     start, payload = call(pack_body, [(row_shape, f32), ((brick_rows, TILE), f32)], rhs, place, polar)
 
@@ -1256,24 +1299,31 @@
     message, near = join(message, payload)
     arrived = exchange(message, devices)
 
-    def pair_first(first_tile, last_tile, *after):
+    def pair_first(first_tile, last_tile, fields, *after):
         def body(*refs):
-            pair_first_body(first_tile, tile_count, spans, *refs)
-
+            pair_first_body(first_tile, last_tile, tile_count, spans, *refs)
+
+        tiles = last_tile - first_tile
         return pair_call(
             body,
-            [(tile_count * listed * TILE, TILE)] * 2 + [(tile_count * GROUP, TILE)],
-            [(9 * 3 * tile_count, TILE)],
+            [(tile_count * listed * TILE, TILE)] * 2,
+            [(last_tile * GROUP, TILE), (9 * 3 * tile_count, TILE)],
             first_tile,
             last_tile,
             0,
-            [(9 * brick_rows, TILE), (listed * quantities * GROUP, TILE), square, wide, sums],
+            [
+                (9 * brick_rows, TILE),
+                (tiles * listed * quantities * GROUP, TILE),
+                (tiles * 4 * TILE, TILE),
+                (tiles * 3 * RHS * TILE, TILE),
+            ],
             lists,
             *near,
+            *fields,
             after=after,
         )
 
-    early = pair_first(0, EARLY_TILES, message)
+    early = pair_first(0, EARLY_TILES, (), message)
 
     def middle_first(*refs):
         middle_first_body(counts, *refs)
@@ -1287,7 +1337,9 @@
         own_block=1,
     )
     returned = exchange(mixed, devices)
-    first_term, second_term, direct, near = pair_first(EARLY_TILES, tile_count, wave, *early[:3])
+    first_term, second_term, direct, near = pair_first(
+        EARLY_TILES, tile_count, (early[2],), wave, *early[:2]
+    )
 
     def sample(*refs):
         sample_body(devices, *refs)
@@ -1316,18 +1368,17 @@
 
     (direct,) = pair_call(
         pair_second,
+        [],
         [(tile_count * GROUP, TILE)],
-        [],
         0,
         tile_count,
         2,
         [
             (9 * moment_rows, TILE),
-            (listed * 3 * GROUP, TILE),
-            (listed * 3 * RHS * GROUP, TILE),
-            square,
-            wide,
-            sums,
+            (tile_count * listed * 3 * GROUP, TILE),
+            (tile_count * listed * 3 * RHS * GROUP, TILE),
+            (tile_count * 3 * TILE, TILE),
+            (tile_count * 3 * RHS * TILE, TILE),
         ],
         lists,
         near,

time: 101 us -> 102 us (level)
    ppermute x0 -> x4, starting transfers between devices: none -> 11.7 us  [the longest x2 6.85 us: pairwise(): lax.ppermute(source, axis, [(i, (i + 1 if i % 2 else i - 1) % count) for...]
    ppermute x8 -> x4, starting transfers between devices: 14.4 us -> 3.49 us  [shift(): lax.ppermute(source, axis, [(i, (i + step) % count) for i in range(count)])]
    ppermute x8 -> x4, waiting for transfers between devices: 4.34 us -> 4.33 us  [shift(): lax.ppermute(source, axis, [(i, (i + step) % count) for i in range(count)])]
  transfers between devices with their start and end apart: 11 -> 11, of which waited for: 2 -> 3; matrix products, arithmetic and copies ran while one was open for 1% -> 1% of each run, Pallas kernels for 33% -> 34%
where the time goes in v1:
time: 102 us; the launch traced here: 101 us
  Pallas kernels  46.7 us (46%)
  starting transfers between devices  28.9 us (28%)
  blocking collectives  15.4 us (15%)
  local copies, waits for them, and re-layouts  4.8 us (5%)
  waiting for transfers between devices  4.6 us (5%)
    pallas_call x3, Pallas kernels, pair_call(): pl.pallas_call(body, out_shape=out_shape, grid_spec=pltpu.PrefetchScalarG...  26.2 us
    pallas_call x6, Pallas kernels, call(): pl.pallas_call(run, in_specs=[anywhere()] * (len(after) + count), out_spe...  19 us
    all_to_all x1, blocking collectives, exchange(): lax.all_to_all(sent, ('row', 'col'), split_axis=0, concat_axis=0, tiled=T...  15.4 us
    all_to_all x3, starting transfers between devices, exchange(): lax.all_to_all(sent, ('row', 'col'), split_axis=0, concat_axis=0, tiled=T...  13.7 us
    ppermute x2, starting transfers between devices, pairwise(): lax.ppermute(source, axis, [(i, (i + 1 if i % 2 else i - 1) % count) for...  6.85 us
    ppermute x2, starting transfers between devices, pairwise(): first = lax.ppermute(source, axis, [(i, i ^ 1) for i in range(count)])  4.86 us
    unnamed x40, local copies, waits for them, and re-layouts  4.79 us
    ppermute x4, waiting for transfers between devices, shift(): lax.ppermute(source, axis, [(i, (i + step) % count) for i in range(count)])  4.33 us
  transfers between devices with their start and end apart: 11, of which 3 were waited for; matrix products, arithmetic and copies ran while one was open for 1% of the time, Pallas kernels for 34%

profile of v1, /device:TPU:0, one launch (start us, length us, event | category | flops | bytes accessed | tf_op | source)
XLA Modules:
  0.0 101.3 jit_solution(9212916219392932640)
XLA Ops:
  0.6 1.4 %shard_map.131 = (f32[6,512]{1,0:T(8,128)}, f32[40,128]{1,0:T(8,128)}) custom-call(f32[3,2,512]{2,1,0:T(2,128)} %bitcast.22, f32[3,1,512]{2,1,0:T(1,128)} %bitcast.41, f32[1,512]{1,0:T(1,128)} %bitcast.25), custom_call_target="tpu_custom_call" | custom-call | flops 200000000 | bytes 4194304 | tf_op jit(solution)/shard_map/pallas_call | solution.py:1183
  2.0 3.0 %collective-permute-start.1 = (f32[40,128]{1,0:T(8,128)}, f32[40,128]{1,0:T(8,128)S(1)}, u32[]{:S(2)}, u32[]{:S(2)}) collective-permute-start(f32[40,128]{1,0:T(8,128)} %get-tuple-element.33), channel_id=1, source_target_pairs={{0,1},{1,0},{2,3},{3,2},{4,5},{5,4},{6,7},{7,6},{8,9},{9,8},{10,11... | collective-permute-start | bytes 61448 | tf_op jit(solution)/shard_map/ppermute | solution.py:1119
  5.1 3.5 %collective-permute-start = (f32[40,128]{1,0:T(8,128)}, f32[40,128]{1,0:T(8,128)S(1)}, u32[]{:S(2)}, u32[]{:S(2)}) collective-permute-start(f32[40,128]{1,0:T(8,128)} %get-tuple-element.33), channel_id=1, source_target_pairs={{0,7},{1,2},{2,1},{3,4},{4,3},{5,6},{6,5},{7,0},{8,15},{9,10},{10,... | collective-permute-start | bytes 61448 | tf_op jit(solution)/shard_map/ppermute | solution.py:1120
  8.6 5.0 %shard_map.132 = (f32[384,128]{1,0:T(8,128)}, f32[48,512]{1,0:T(8,128)}, bf16[256,1024]{1,0:T(8,128)(2,1)}, bf16[256,1024]{1,0:T(8,128)(2,1)}) custom-call(f32[3,1,512]{2,1,0:T(1,128)} %bitcast.42, s32[3,1,512]{2,1,0:T(1,128)} %bitcast.43, f32[6,512]{1,0:T(8,128)} %get-tuple-element.28.refs_2_.refs_4_.refs_8_.refs_5_, ...), custom_call_target="tpu_custom_call" | custom-call | flops 200000000 | bytes 4194304 | tf_op jit(solution)/shard_map/pallas_call | solution.py:1183
  13.7 2.9 %all-to-all-start = ((f32[32,1,1536]{2,1,0:T(1,128)}), f32[32,1,1536]{2,1,0:T(1,128)S(1)}, u32[]{:S(2)}, u32[]{:S(2)}) async-start(f32[32,1,1536]{2,1,0:T(1,128)} %bitcast.34), calls=%async_computation | async-start | bytes 393216 | tf_op jit(solution)/shard_map/all_to_all | solution.py:1246
  16.6 0.7 constant_dynamic-update-slice_fusion.1
  17.4 0.3 collective-permute-start.2
  17.6 1.5 %collective-permute-start.3 = (f32[120,128]{1,0:T(8,128)S(1)}, f32[120,128]{1,0:T(8,128)S(1)}, u32[]{:S(2)}, u32[]{:S(2)}) collective-permute-start(f32[120,128]{1,0:T(8,128)S(1)} %constant_dynamic-update-slice_fusion.refs_2_), channel_id=1, source_target_pairs={{0,24},{8,0},{16,8},{24,16},{1,25},{9,1},{17,9},{25,17},{2,26},{10... | collective-permute-start | bytes 184328 | tf_op jit(solution)/shard_map/ppermute | solution.py:1102
  19.1 2.4 %collective-permute-done.2.refs_1_ = f32[120,128]{1,0:T(8,128)S(1)} collective-permute-done((f32[120,128]{1,0:T(8,128)S(1)}, f32[120,128]{1,0:T(8,128)S(1)}, u32[]{:S(2)}, u32[]{:S(2)}) %collective-permute-start.2) | collective-permute-done | bytes 61472 | tf_op jit(solution)/shard_map/ppermute | solution.py:1102
  21.5 0.6 copy-done.14
  22.2 5.5 %shard_map.133 = (f32[6144,128]{1,0:T(8,128)}, f32[6144,128]{1,0:T(8,128)}, f32[8,128]{1,0:T(8,128)}, f32[108,128]{1,0:T(8,128)}) custom-call(s32[4,12]{1,0:T(4,128)} %bitcast.36, f32[120,128]{1,0:T(8,128)} %copy-done.14, f32[120,128]{1,0:T(8,128)} %copy-done.12, f32[120,128]{1,0:T(8,128)} %copy-done.15, f32[384,128]{1,0:T(8,128)} %get-tuple-element.36.refs_4_), custom_call_target="tpu_custom_call" | custom-call | flops 80000000 | bytes 8388608 | tf_op jit(solution)/shard_map/pallas_call | solution.py:1222
  27.7 0.7 copy-done.9
  28.4 3.1 %shard_map.134 = (f32[384,128]{1,0:T(8,128)}, f32[64,256]{1,0:T(8,128)}) custom-call(f32[8,128]{1,0:T(8,128)} %get-tuple-element.37.refs_0_.refs_4_, f32[384,128]{1,0:T(8,128)} %bitcast.30, f32[32,64,256]{2,1,0:T(8,128)} %constant.26.clone.refs_2_.refs_1_, bf16[32,144]{1,0:T(8,128)(2,1)} %constant.27.clone.refs_3_.refs_2_, ...), custom_call_target="tpu_custom_call" | custom-call | flops 200000000 | bytes 4194304 | tf_op jit(solution)/shard_map/pallas_call | solution.py:1183
  31.5 6.2 %all-to-all-start.1 = ((f32[32,1,1536]{2,1,0:T(1,128)}), f32[32,1,1536]{2,1,0:T(1,128)S(1)}, u32[]{:S(2)}, u32[]{:S(2)}) async-start(f32[32,1,1536]{2,1,0:T(1,128)} %bitcast.35), calls=%async_computation.1 | async-start | bytes 393216 | tf_op jit(solution)/shard_map/all_to_all | solution.py:1246
  37.7 11.6 %shard_map.135 = (f32[6144,128]{1,0:T(8,128)}, f32[6144,128]{1,0:T(8,128)}, f32[32,128]{1,0:T(8,128)}, f32[108,128]{1,0:T(8,128)}) custom-call(s32[4,12]{1,0:T(4,128)} %bitcast.37, f32[120,128]{1,0:T(8,128)} %copy-done.14, f32[120,128]{1,0:T(8,128)} %copy-done.12, f32[120,128]{1,0:T(8,128)} %copy-done.15, ...), custom_call_target="tpu_custom_call", output_to_operand_aliasing={{0}: (6, {}), {1}: (7, {})} | custom-call | flops 80000000 | bytes 8388608 | tf_op jit(solution)/shard_map/pallas_call | solution.py:1222
  49.3 0.7 copy-done.10
  50.0 3.0 %shard_map.136 = (f32[6,512]{1,0:T(8,128)}, f32[6,512]{1,0:T(8,128)}, f32[24,128]{1,0:T(8,128)}) custom-call(f32[384,128]{1,0:T(8,128)} %bitcast.32, f32[48,512]{1,0:T(8,128)} %get-tuple-element.29.refs_1_.refs_0_, bf16[256,1024]{1,0:T(8,128)(2,1)} %get-tuple-element.30.refs_2_.refs_1_, bf16[256,1024]{1,0:T(8,128)(2,1)} %get-tuple-element.31.refs_3_.refs_2_, ...), custom_call_target="tpu_custom_call" | custom-call | flops 200000000 | bytes 4194304 | tf_op jit(solution)/shard_map/pallas_call | solution.py:1183
  53.0 1.8 %collective-permute-start.5 = (f32[24,128]{1,0:T(8,128)}, f32[24,128]{1,0:T(8,128)S(1)}, u32[]{:S(2)}, u32[]{:S(2)}) collective-permute-start(f32[24,128]{1,0:T(8,128)} %get-tuple-element.44), channel_id=1, source_target_pairs={{0,1},{1,0},{2,3},{3,2},{4,5},{5,4},{6,7},{7,6},{8,9},{9,8},{10,11... | collective-permute-start | bytes 36872 | tf_op jit(solution)/shard_map/ppermute | solution.py:1119
  54.9 3.3 %collective-permute-start.4 = (f32[24,128]{1,0:T(8,128)}, f32[24,128]{1,0:T(8,128)S(1)}, u32[]{:S(2)}, u32[]{:S(2)}) collective-permute-start(f32[24,128]{1,0:T(8,128)} %get-tuple-element.44), channel_id=1, source_target_pairs={{0,7},{1,2},{2,1},{3,4},{4,3},{5,6},{6,5},{7,0},{8,15},{9,10},{10,... | collective-permute-start | bytes 36872 | tf_op jit(solution)/shard_map/ppermute | solution.py:1120
  58.2 3.0 %shard_map.137 = f32[384,128]{1,0:T(8,128)} custom-call(f32[48,512]{1,0:T(8,128)} %get-tuple-element.29.refs_1_.refs_0_, bf16[256,1024]{1,0:T(8,128)(2,1)} %get-tuple-element.30.refs_2_.refs_1_, bf16[256,1024]{1,0:T(8,128)(2,1)} %get-tuple-element.31.refs_3_.refs_2_, f32[6,512]{1,0:T(8,128)} %get-tuple-element.43.refs_3_.refs_10_.refs_7_), custom_call_target="tpu_custom_call" | custom-call | flops 200000000 | bytes 4194304 | tf_op jit(solution)/shard_map/pallas_call | solution.py:1183
  61.2 0.3 collective-permute-done.4
  61.5 4.6 %all-to-all-start.2 = ((f32[32,1,1536]{2,1,0:T(1,128)}), f32[32,1,1536]{2,1,0:T(1,128)S(1)}, u32[]{:S(2)}, u32[]{:S(2)}) async-start(f32[32,1,1536]{2,1,0:T(1,128)} %bitcast.31), calls=%async_computation.2 | async-start | bytes 393216 | tf_op jit(solution)/shard_map/all_to_all | solution.py:1246
  66.1 0.7 constant_dynamic-update-slice_fusion.4
  66.8 0.3 collective-permute-start.6
  67.1 1.5 %collective-permute-start.7 = (f32[72,128]{1,0:T(8,128)S(1)}, f32[72,128]{1,0:T(8,128)S(1)}, u32[]{:S(2)}, u32[]{:S(2)}) collective-permute-start(f32[72,128]{1,0:T(8,128)S(1)} %constant_dynamic-update-slice_fusion.3.refs_3_), channel_id=1, source_target_pairs={{0,24},{8,0},{16,8},{24,16},{1,25},{9,1},{17,9},{25,17},{2,26},{10... | collective-permute-start | bytes 110600 | tf_op jit(solution)/shard_map/ppermute | solution.py:1102
  68.6 1.9 %collective-permute-done.6.refs_2_ = f32[72,128]{1,0:T(8,128)S(1)} collective-permute-done((f32[72,128]{1,0:T(8,128)S(1)}, f32[72,128]{1,0:T(8,128)S(1)}, u32[]{:S(2)}, u32[]{:S(2)}) %collective-permute-start.6) | collective-permute-done | bytes 36896 | tf_op jit(solution)/shard_map/ppermute | solution.py:1102
  70.5 0.6 copy-done.16
  71.1 9.0 %shard_map.138.refs_11_.refs_8_ = f32[32,128]{1,0:T(8,128)} custom-call(s32[4,12]{1,0:T(4,128)} %bitcast.38, f32[108,128]{1,0:T(8,128)} %get-tuple-element.47.refs_1_, f32[72,128]{1,0:T(8,128)} %copy-done.16, f32[72,128]{1,0:T(8,128)} %copy-done.13, f32[72,128]{1,0:T(8,128)} %copy-done.17, f32[6144,128]{1,0:T(8,128)} %get-tuple-element.50.refs_5_, ...), custom_call_target="tpu_custom_call" | custom-call | flops 80000000 | bytes 8388608 | tf_op jit(solution)/shard_map/pallas_call | solution.py:1222
  80.2 0.7 copy-done.11
  80.9 3.4 %shard_map.139 = f32[416,128]{1,0:T(8,128)} custom-call(f32[384,128]{1,0:T(8,128)} %bitcast.33, f32[32,64,256]{2,1,0:T(8,128)} %constant.26.clone.refs_2_.refs_1_, bf16[32,144]{1,0:T(8,128)(2,1)} %constant.27.clone.refs_3_.refs_2_, bf16[48,96]{1,0:T(8,128)(2,1)} %constant.28.clone.refs_4_.refs_3_, bf16[512,256]{1,0:T(8,128)(2,1)} %constant.29.clone.refs_5_.refs_4_, ...), custom_call_target="tpu_custom_call" | custom-call | flops 200000000 | bytes 4194304 | tf_op jit(solution)/shard_map/pallas_call | solution.py:1183
  84.3 15.4 %all_to_all.20 = f32[32,1,1664]{2,1,0:T(1,128)S(1)} all-to-all(f32[32,1,1664]{2,1,0:T(1,128)} %bitcast.29), channel_id=1, replica_groups=mesh['row'=4,'col'=8] {'row','col'}, dimensions={0} | all-to-all | bytes 425984 | tf_op jit(solution)/shard_map/all_to_all | solution.py:1246
  99.8 1.5 %shard_map.140 = (f32[3,2,512]{2,1,0:T(2,128)}, f32[3,2,512]{2,1,0:T(2,128)}) custom-call(f32[416,128]{1,0:T(8,128)S(1)} %bitcast.21, f32[48,512]{1,0:T(8,128)S(1)} %copy-done.2, bf16[256,1024]{1,0:T(8,128)(2,1)S(1)} %copy-done, bf16[256,1024]{1,0:T(8,128)(2,1)S(1)} %copy-done.1, f32[3,2,512]{2,1,0:T(2,128)S(1)} %bitcast.24, f32[6,512]{1,0:T(8,128)S(1)} %copy-done.3, ...), custom_call_target="tpu_custom_call" | custom-call | tf_op jit(solution)/shard_map/pallas_call | solution.py:1199
  (45 shorter events, 0.1 us)
Async XLA Ops:
  2.0 11.6 %collective-permute-start.1 = (f32[40,128]{1,0:T(8,128)}, f32[40,128]{1,0:T(8,128)S(1)}, u32[]{:S(2)}, u32[]{:S(2)}) collective-permute-start(f32[40,128]{1,0:T(8,128)} %get-tuple-element.33), channel_id=1, source_target_pairs={{0,1},{1,0},{2,3},{3,2},{4,5},{5,4},{6,7},{7,6},{8,9},{9,8},{10,11... | collective-permute-start | bytes 61448 | tf_op jit(solution)/shard_map/ppermute | solution.py:1119
  5.1 8.6 %collective-permute-start = (f32[40,128]{1,0:T(8,128)}, f32[40,128]{1,0:T(8,128)S(1)}, u32[]{:S(2)}, u32[]{:S(2)}) collective-permute-start(f32[40,128]{1,0:T(8,128)} %get-tuple-element.33), channel_id=1, source_target_pairs={{0,7},{1,2},{2,1},{3,4},{4,3},{5,6},{6,5},{7,0},{8,15},{9,10},{10,... | collective-permute-start | bytes 61448 | tf_op jit(solution)/shard_map/ppermute | solution.py:1120
  13.7 14.0 %all-to-all-start = ((f32[32,1,1536]{2,1,0:T(1,128)}), f32[32,1,1536]{2,1,0:T(1,128)S(1)}, u32[]{:S(2)}, u32[]{:S(2)}) async-start(f32[32,1,1536]{2,1,0:T(1,128)} %bitcast.34), calls=%async_computation | async-start | bytes 393216 | tf_op jit(solution)/shard_map/all_to_all | solution.py:1246
  17.4 4.2 %copy-start.12 = (f32[120,128]{1,0:T(8,128)}, f32[120,128]{1,0:T(8,128)S(1)}, u32[]{:S(2)}) copy-start(f32[120,128]{1,0:T(8,128)S(1)} %constant_dynamic-update-slice_fusion.refs_2_) | copy-start | bytes 184324
  17.4 4.2 %collective-permute-start.2 = (f32[120,128]{1,0:T(8,128)S(1)}, f32[120,128]{1,0:T(8,128)S(1)}, u32[]{:S(2)}, u32[]{:S(2)}) collective-permute-start(f32[120,128]{1,0:T(8,128)S(1)} %constant_dynamic-update-slice_fusion.refs_2_), channel_id=1, source_target_pairs={{0,8},{8,16},{16,24},{24,0},{1,9},{9,17},{17,25},{25,1},{2,10},{10... | collective-permute-start | bytes 184328 | tf_op jit(solution)/shard_map/ppermute | solution.py:1102
  17.6 3.9 %collective-permute-start.3 = (f32[120,128]{1,0:T(8,128)S(1)}, f32[120,128]{1,0:T(8,128)S(1)}, u32[]{:S(2)}, u32[]{:S(2)}) collective-permute-start(f32[120,128]{1,0:T(8,128)S(1)} %constant_dynamic-update-slice_fusion.refs_2_), channel_id=1, source_target_pairs={{0,24},{8,0},{16,8},{24,16},{1,25},{9,1},{17,9},{25,17},{2,26},{10... | collective-permute-start | bytes 184328 | tf_op jit(solution)/shard_map/ppermute | solution.py:1102
  21.5 0.6 copy-start.14
  21.5 0.6 copy-start.15
  27.7 0.7 copy-start.9
  31.5 17.8 %all-to-all-start.1 = ((f32[32,1,1536]{2,1,0:T(1,128)}), f32[32,1,1536]{2,1,0:T(1,128)S(1)}, u32[]{:S(2)}, u32[]{:S(2)}) async-start(f32[32,1,1536]{2,1,0:T(1,128)} %bitcast.35), calls=%async_computation.1 | async-start | bytes 393216 | tf_op jit(solution)/shard_map/all_to_all | solution.py:1246
  49.3 0.7 copy-start.10
  53.0 8.2 %collective-permute-start.5 = (f32[24,128]{1,0:T(8,128)}, f32[24,128]{1,0:T(8,128)S(1)}, u32[]{:S(2)}, u32[]{:S(2)}) collective-permute-start(f32[24,128]{1,0:T(8,128)} %get-tuple-element.44), channel_id=1, source_target_pairs={{0,1},{1,0},{2,3},{3,2},{4,5},{5,4},{6,7},{7,6},{8,9},{9,8},{10,11... | collective-permute-start | bytes 36872 | tf_op jit(solution)/shard_map/ppermute | solution.py:1119
  54.9 6.6 %collective-permute-start.4 = (f32[24,128]{1,0:T(8,128)}, f32[24,128]{1,0:T(8,128)S(1)}, u32[]{:S(2)}, u32[]{:S(2)}) collective-permute-start(f32[24,128]{1,0:T(8,128)} %get-tuple-element.44), channel_id=1, source_target_pairs={{0,7},{1,2},{2,1},{3,4},{4,3},{5,6},{6,5},{7,0},{8,15},{9,10},{10,... | collective-permute-start | bytes 36872 | tf_op jit(solution)/shard_map/ppermute | solution.py:1120
  61.5 18.7 %all-to-all-start.2 = ((f32[32,1,1536]{2,1,0:T(1,128)}), f32[32,1,1536]{2,1,0:T(1,128)S(1)}, u32[]{:S(2)}, u32[]{:S(2)}) async-start(f32[32,1,1536]{2,1,0:T(1,128)} %bitcast.31), calls=%async_computation.2 | async-start | bytes 393216 | tf_op jit(solution)/shard_map/all_to_all | solution.py:1246
  66.8 3.7 %copy-start.13 = (f32[72,128]{1,0:T(8,128)}, f32[72,128]{1,0:T(8,128)S(1)}, u32[]{:S(2)}) copy-start(f32[72,128]{1,0:T(8,128)S(1)} %constant_dynamic-update-slice_fusion.3.refs_3_) | copy-start | bytes 110596
  66.8 3.6 %collective-permute-start.6 = (f32[72,128]{1,0:T(8,128)S(1)}, f32[72,128]{1,0:T(8,128)S(1)}, u32[]{:S(2)}, u32[]{:S(2)}) collective-permute-start(f32[72,128]{1,0:T(8,128)S(1)} %constant_dynamic-update-slice_fusion.3.refs_3_), channel_id=1, source_target_pairs={{0,8},{8,16},{16,24},{24,0},{1,9},{9,17},{17,25},{25,1},{2,10},{10... | collective-permute-start | bytes 110600 | tf_op jit(solution)/shard_map/ppermute | solution.py:1102
  67.1 3.4 %collective-permute-start.7 = (f32[72,128]{1,0:T(8,128)S(1)}, f32[72,128]{1,0:T(8,128)S(1)}, u32[]{:S(2)}, u32[]{:S(2)}) collective-permute-start(f32[72,128]{1,0:T(8,128)S(1)} %constant_dynamic-update-slice_fusion.3.refs_3_), channel_id=1, source_target_pairs={{0,24},{8,0},{16,8},{24,16},{1,25},{9,1},{17,9},{25,17},{2,26},{10... | collective-permute-start | bytes 110600 | tf_op jit(solution)/shard_map/ppermute | solution.py:1102
  70.5 0.6 copy-start.16
  70.5 0.6 copy-start.17
  80.1 19.6 %copy-start = (bf16[256,1024]{1,0:T(8,128)(2,1)S(1)}, bf16[256,1024]{1,0:T(8,128)(2,1)}, u32[]{:S(2)}) copy-start(bf16[256,1024]{1,0:T(8,128)(2,1)} %get-tuple-element.30.refs_2_.refs_1_) | copy-start | bytes 1572868
  80.1 19.6 %copy-start.1 = (bf16[256,1024]{1,0:T(8,128)(2,1)S(1)}, bf16[256,1024]{1,0:T(8,128)(2,1)}, u32[]{:S(2)}) copy-start(bf16[256,1024]{1,0:T(8,128)(2,1)} %get-tuple-element.31.refs_3_.refs_2_) | copy-start | bytes 1572868
  80.1 19.6 %copy-start.2 = (f32[48,512]{1,0:T(8,128)S(1)}, f32[48,512]{1,0:T(8,128)}, u32[]{:S(2)}) copy-start(f32[48,512]{1,0:T(8,128)} %get-tuple-element.29.refs_1_.refs_0_) | copy-start | bytes 294916
  80.1 19.6 %copy-start.3 = (f32[6,512]{1,0:T(8,128)S(1)}, f32[6,512]{1,0:T(8,128)}, u32[]{:S(2)}) copy-start(f32[6,512]{1,0:T(8,128)} %get-tuple-element.28.refs_2_.refs_4_.refs_8_.refs_5_) | copy-start | bytes 36868
  80.1 19.6 %copy-start.4 = (f32[6,512]{1,0:T(8,128)S(1)}, f32[6,512]{1,0:T(8,128)}, u32[]{:S(2)}) copy-start(f32[6,512]{1,0:T(8,128)} %get-tuple-element.43.refs_3_.refs_10_.refs_7_) | copy-start | bytes 36868
  80.1 19.6 %copy-start.5 = (f32[32,128]{1,0:T(8,128)S(1)}, f32[32,128]{1,0:T(8,128)}, u32[]{:S(2)}) copy-start(f32[32,128]{1,0:T(8,128)} %shard_map.138.refs_11_.refs_8_) | copy-start | bytes 49156
  80.2 19.6 %copy-start.6 = (f32[6,512]{1,0:T(8,128)S(1)}, f32[6,512]{1,0:T(8,128)}, u32[]{:S(2)}) copy-start(f32[6,512]{1,0:T(8,128)} %get-tuple-element.46.refs_9_.refs_6_) | copy-start | bytes 36868
  80.2 19.6 %copy-start.7 = (f32[1,1,2,3,512]{4,2,3,1,0:T(2,128)S(1)}, f32[1,1,2,3,512]{4,2,3,1,0:T(2,128)}, u32[]{:S(2)}) copy-start(f32[1,1,2,3,512]{4,2,3,1,0:T(2,128)} %param.12) | copy-start | bytes 36868
  80.2 19.6 %copy-start.8 = (f32[1,1,512]{2,1,0:T(1,128)S(1)}, f32[1,1,512]{2,1,0:T(1,128)}, u32[]{:S(2)}) copy-start(f32[1,1,512]{2,1,0:T(1,128)} %param.14) | copy-start | bytes 6148
  80.2 0.7 copy-start.11
